TPU v7x, 256 devices: a whole 4x4x8 slice. The times are simulated.
256 devices in a mesh: gz: 16 (over y, x), gy: 2 (over z_lo), af: 8 (over z_hi, core).
Axes of the slice: x: 4, y: 4, z: 8 (z_hi: 4, z_lo: 2; z = z_hi * 2 + z_lo), core: 2. Of those that a mesh axis runs over, the one named last changes fastest.
Arguments:
- features: bfloat16 [256, 32, 1024], P('af', 'gz', 'gy'), may hold values from -6 to 6
- filters: bfloat16 [3, 3, 3, 256, 256], P(None, None, None, 'af'), may hold values from -0.078125 to 0.078125
- cotangent: bfloat16 [256, 32, 1024], P('af', 'gz', 'gy'), may hold values from -6 to 6
Outputs:
- response: bfloat16 [256, 32, 1024], P('af', 'gz', 'gy')
- input_grad: bfloat16 [256, 32, 1024], P('af', 'gz', 'gy')
- filter_grad: float32 [3, 3, 3, 256, 256], P(None, None, None, 'af')
All inputs are finite; a program needn't handle non-finite values.
Results may differ from a plain program's by a relative error of at most 0.0013.
Values may be sent and summed in bfloat16 or wider, within the bound.
A program may use at most 64 MiB of HBM per device.

v0:
```python
import jax
import jax.numpy as jnp
from jax import lax
from jax.sharding import PartitionSpec as P

WIDTH = 64


def extended(cells, sides, width):
    for axis, dim in sides:
        count = lax.axis_size(axis)
        ends = count - 1
        head = lax.slice_in_dim(cells, 0, width, axis=dim)
        tail = lax.slice_in_dim(cells, cells.shape[dim] - width, cells.shape[dim], axis=dim)
        cells = jnp.concatenate(
            [
                lax.ppermute(tail, axis, [(i, (i + 1) % count) for i in range(ends)]),
                cells,
                lax.ppermute(head, axis, [((i + 1) % count, i) for i in range(ends)]),
            ],
            axis=dim,
        )
    return cells


def variants(padded, width):
    flat = padded.shape[2]
    column = lax.iota(jnp.int32, flat) % width
    zero = jnp.zeros((), padded.dtype)
    left = jnp.where(column == width - 1, zero, padded)
    right = jnp.where(column == 0, zero, padded)
    result = []
    for member in (left, padded, right):
        result.append(jnp.pad(member, ((0, 0), (0, 0), (1, 1))))
    return result


def window(sources, offs, depth, span, width):
    a, b, c = offs
    source = sources[c + 1]
    start = 1 + (1 + b) * width + c
    return lax.slice_in_dim(
        lax.slice_in_dim(source, 1 + a, 1 + a + depth, axis=1), start, start + span, axis=2
    )


def apply_taps(sources, tap_weight, form, sign, depth, span, width):
    total = None
    for tz in range(3):
        for ty in range(3):
            for tx in range(3):
                offs = (sign * (tz - 1), sign * (ty - 1), sign * (tx - 1))
                piece = window(sources, offs, depth, span, width)
                term = jnp.einsum(
                    form, tap_weight(tz, ty, tx), piece, preferred_element_type=jnp.float32
                )
                total = term if total is None else total + term
    return total


def shards(features, filters, cotangent):
    depth = features.shape[1]
    span = features.shape[2]
    whole = lax.all_gather(features, "af", axis=0, tiled=True)
    deep = extended(whole, (("gz", 1),), 1)
    padded = extended(deep, (("gy", 2),), WIDTH)
    field_src = variants(padded, WIDTH)

    def forward_tap(tz, ty, tx):
        return filters[tz, ty, tx]

    response = apply_taps(field_src, forward_tap, "oc,cdp->odp", 1, depth, span, WIDTH).astype(
        jnp.bfloat16
    )
    cot_deep = extended(cotangent, (("gz", 1),), 1)
    cot_pad = extended(cot_deep, (("gy", 2),), WIDTH)
    cot_src = variants(cot_pad, WIDTH)

    def column_tap(tz, ty, tx):
        return filters[tz, ty, tx]

    input_grad = lax.psum_scatter(
        apply_taps(cot_src, column_tap, "oc,odp->cdp", -1, depth, span, WIDTH),
        "af",
        scatter_dimension=0,
        tiled=True,
    ).astype(jnp.bfloat16)
    filter_rows = []
    for tz in range(3):
        for ty in range(3):
            for tx in range(3):
                piece = window(field_src, (tz - 1, ty - 1, tx - 1), depth, span, WIDTH)
                filter_rows.append(
                    jnp.einsum("odp,cdp->oc", cotangent, piece, preferred_element_type=jnp.float32)
                )
    local_grad = jnp.stack(filter_rows).reshape(3, 3, 3, cotangent.shape[0], padded.shape[0])
    summed = lax.psum(local_grad, ("gz", "gy"))
    cells = depth * span * lax.axis_size("gz") * lax.axis_size("gy")
    filter_grad = summed * (1.0 / jnp.sqrt(jnp.float32(cells)))
    return (response, input_grad, filter_grad)


def solution(mesh):
    placed = (P("af", "gz", "gy"), P(None, None, None, "af", None), P("af", "gz", "gy"))
    return jax.shard_map(
        shards,
        mesh=mesh,
        in_specs=placed,
        out_specs=(P("af", "gz", "gy"), P("af", "gz", "gy"), P(None, None, None, "af", None)),
        check_vma=False,
    )
```

profile of v0, /device:TPU:32, one launch (start us, length us, event | category | flops | bytes accessed | tf_op | source)
XLA Modules:
  0.0 474.9 jit_solution(8360042680567663925)
XLA Ops:
  7.2 0.9 copy.44
  8.1 1.3 collective-permute-start.5
  9.4 4.5 collective-permute-start.4
  14.0 0.9 copy.43
  14.8 17.7 %all_gather.3 = bf16[256,2,512]{2,0,1:T(8,128)(2,1)S(1)} all-gather(bf16[32,2,512]{2,0,1:T(8,128)(2,1)S(1)} %copy.43), channel_id=1, replica_groups=mesh['gz'=16,'gy'=2,'af'=8] {'af'}, dimensions={0}, use_global_device_ids=true | all-gather | bytes 589824 | tf_op jit(solution)/shard_map/all_gather | solution.py:64
  32.5 0.8 fusion.326
  33.3 1.3 collective-permute-start.1
  34.6 5.3 %collective-permute-start = (bf16[256,1,512]{2,0,1:T(8,128)(2,1)}, bf16[256,1,512]{2,0,1:T(8,128)(2,1)}, u32[]{:S(2)}, u32[]{:S(2)}) collective-permute-start(bf16[256,1,512]{2,0,1:T(8,128)(2,1)} %get-tuple-element.17), channel_id=1, source_target_pairs={{0,16},{16,32},{32,48},{48,64},{64,80},{80,96},{96,112},{112,128},... | collective-permute-start | bytes 786440 | tf_op jit(solution)/shard_map/ppermute | solution.py:17
  40.5 1.3 collective-permute-start.6
  41.8 4.5 collective-permute-start.7
  48.1 1.1 convolution_bitcast_fusion.3
  49.2 1.2 fusion.141
  50.5 1.1 fusion.128
  61.4 1.5 fusion.18
  63.0 1.5 copy.51
  64.5 58.5 %all-reduce.9 = bf16[256,2,512]{2,1,0:T(2,128)(2,1)S(1)} all-reduce(f32[256,2,512]{2,1,0:T(2,128)S(1)} %copy.51), channel_id=2, replica_groups=mesh['gz'=16,'gy'=2,'af'=8] {'af'}, use_global_device_ids=true, to_apply=%region_0.1.clone | all-reduce | flops 262144 | bytes 1572864
  123.8 1.0 constant_dynamic-update-slice_fusion.4
  125.1 1.4 collective-permute-start.2
  126.5 4.8 %collective-permute-start.3 = (bf16[256,4,64]{2,0,1:T(8,128)(2,1)S(1)}, bf16[256,4,64]{2,0,1:T(8,128)(2,1)S(1)}, u32[]{:S(2)}, u32[]{:S(2)}) collective-permute-start(bf16[256,4,64]{2,0,1:T(8,128)(2,1)S(1)} %get-tuple-element.12), channel_id=1, source_target_pairs={{8,0},{9,1},{10,2},{11,3},{12,4},{13,5},{14,6},{15,7},{24,16},{25,... | collective-permute-start | bytes 393224 | tf_op jit(solution)/shard_map/ppermute | solution.py:19
  131.5 2.5 collective-permute-done.2
  134.1 1.2 collective-permute-done.3
  135.3 1.0 broadcast_select_fusion.1
  138.0 1.0 convolution_bitcast_fusion.16
  144.4 1.0 fusion.24
  154.3 0.9 copy-done.6
  155.2 1.2 convolution_bitcast_fusion.13
  156.4 1.3 fusion.23
  157.7 1.1 fusion.21
  158.7 1.1 fusion.32
  159.8 0.7 copy.79
  160.5 305.3 %all-reduce.8.cloned.1.call-done = f32[3,3,3,32,256]{4,3,2,1,0:T(8,128)} async-done(((f32[3,3,3,32,256]{4,3,2,1,0:T(8,128)}), f32[3,3,3,32,256]{4,3,2,1,0:T(8,128)}) %all-reduce.8.cloned.1.call-update) | async-done | bytes 884752 | tf_op jit(solution)/shard_map/psum | solution.py:97
  465.8 2.2 broadcast_multiply_fusion
  (118 shorter events, 28.6 us)
Async XLA Ops:
  7.2 39.2 %copy-start.13 = (u32[256]{0:T(256)S(1)}, u32[256]{0:T(256)}, u32[]{:S(2)}) copy-start(u32[256]{0:T(256)} %constant.39) | copy-start | bytes 3076
  7.2 32.7 %copy-start.2 = (bf16[32,2,512]{2,1,0:T(2,128)(2,1)S(1)}, bf16[32,2,512]{2,1,0:T(2,128)(2,1)}, u32[]{:S(2)}) copy-start(bf16[32,2,512]{2,1,0:T(2,128)(2,1)} %param.5) | copy-start | bytes 196612
  7.2 458.7 %all-reduce.8.cloned.1.call-start = ((), (), s32[]{:S(2)}) async-start(), calls=%async_computation | async-start | bytes 1769472 | tf_op jit(solution)/shard_map/psum | solution.py:97
  8.1 31.8 %collective-permute-start.5 = (bf16[32,1,512]{2,0,1:T(8,128)(2,1)S(1)}, bf16[32,1,512]{2,0,1:T(8,128)(2,1)S(1)}, u32[]{:S(2)}, u32[]{:S(2)}) collective-permute-start(bf16[32,1,512]{2,0,1:T(8,128)(2,1)S(1)} %get-tuple-element.26), channel_id=1, source_target_pairs={{16,0},{32,16},{48,32},{64,48},{80,64},{96,80},{112,96},{128,112},... | collective-permute-start | bytes 98312 | tf_op jit(solution)/shard_map/ppermute | solution.py:19
  9.4 30.4 %collective-permute-start.4 = (bf16[32,1,512]{2,0,1:T(8,128)(2,1)S(1)}, bf16[32,1,512]{2,0,1:T(8,128)(2,1)S(1)}, u32[]{:S(2)}, u32[]{:S(2)}) collective-permute-start(bf16[32,1,512]{2,0,1:T(8,128)(2,1)S(1)} %get-tuple-element.27), channel_id=1, source_target_pairs={{0,16},{16,32},{32,48},{48,64},{64,80},{80,96},{96,112},{112,128},... | collective-permute-start | bytes 98312 | tf_op jit(solution)/shard_map/ppermute | solution.py:17
  33.3 91.6 %collective-permute-start.1 = (bf16[256,1,512]{2,0,1:T(8,128)(2,1)}, bf16[256,1,512]{2,0,1:T(8,128)(2,1)S(1)}, u32[]{:S(2)}, u32[]{:S(2)}) collective-permute-start(bf16[256,1,512]{2,0,1:T(8,128)(2,1)} %get-tuple-element.16), channel_id=1, source_target_pairs={{16,0},{32,16},{48,32},{64,48},{80,64},{96,80},{112,96},{128,112},... | collective-permute-start | bytes 786440 | tf_op jit(solution)/shard_map/ppermute | solution.py:19
  34.6 89.2 %collective-permute-start = (bf16[256,1,512]{2,0,1:T(8,128)(2,1)}, bf16[256,1,512]{2,0,1:T(8,128)(2,1)}, u32[]{:S(2)}, u32[]{:S(2)}) collective-permute-start(bf16[256,1,512]{2,0,1:T(8,128)(2,1)} %get-tuple-element.17), channel_id=1, source_target_pairs={{0,16},{16,32},{32,48},{48,64},{64,80},{80,96},{96,112},{112,128},... | collective-permute-start | bytes 786440 | tf_op jit(solution)/shard_map/ppermute | solution.py:17
  39.9 2.0 copy-start.9
  39.9 0.6 copy-start.11
  40.5 7.1 %collective-permute-start.6 = (bf16[32,4,64]{2,0,1:T(8,128)(2,1)S(1)}, bf16[32,4,64]{2,0,1:T(8,128)(2,1)S(1)}, u32[]{:S(2)}, u32[]{:S(2)}) collective-permute-start(bf16[32,4,64]{2,0,1:T(8,128)(2,1)S(1)} %get-tuple-element.24), channel_id=1, source_target_pairs={{0,8},{1,9},{2,10},{3,11},{4,12},{5,13},{6,14},{7,15},{16,24},{17,... | collective-permute-start | bytes 49160 | tf_op jit(solution)/shard_map/ppermute | solution.py:17
  41.8 6.1 %collective-permute-start.7 = (bf16[32,4,64]{2,0,1:T(8,128)(2,1)S(1)}, bf16[32,4,64]{2,0,1:T(8,128)(2,1)S(1)}, u32[]{:S(2)}, u32[]{:S(2)}) collective-permute-start(bf16[32,4,64]{2,0,1:T(8,128)(2,1)S(1)} %get-tuple-element.25), channel_id=1, source_target_pairs={{8,0},{9,1},{10,2},{11,3},{12,4},{13,5},{14,6},{15,7},{24,16},{25,... | collective-permute-start | bytes 49160 | tf_op jit(solution)/shard_map/ppermute | solution.py:19
  49.2 2.4 copy-start.4
  55.0 0.9 copy-start.12
  60.6 0.9 copy-start.10
  124.9 6.5 %copy-start.5 = (bf16[3,3,3,32,256]{4,3,2,1,0:T(8,128)(2,1)S(1)}, bf16[3,3,3,32,256]{4,3,2,1,0:T(8,128)(2,1)}, u32[]{:S(2)}) copy-start(bf16[3,3,3,32,256]{4,3,2,1,0:T(8,128)(2,1)} %param.4) | copy-start | bytes 1327108
  125.0 27.6 %copy-start.3 = (bf16[256,3,512]{2,0,1:T(8,128)(2,1)}, bf16[256,3,512]{2,0,1:T(8,128)(2,1)S(1)}, u32[]{:S(2)}) copy-start(bf16[256,3,512]{2,0,1:T(8,128)(2,1)S(1)} %get-tuple-element.18) | copy-start | bytes 2359300
  125.0 28.6 %copy-start = (bf16[256,4,512]{2,0,1:T(8,128)(2,1)}, bf16[256,4,512]{2,0,1:T(8,128)(2,1)S(1)}, u32[]{:S(2)}) copy-start(bf16[256,4,512]{2,0,1:T(8,128)(2,1)S(1)} %get-tuple-element.19) | copy-start | bytes 3145732
  125.1 9.0 %collective-permute-start.2 = (bf16[256,4,64]{2,0,1:T(8,128)(2,1)S(1)}, bf16[256,4,64]{2,0,1:T(8,128)(2,1)S(1)}, u32[]{:S(2)}, u32[]{:S(2)}) collective-permute-start(bf16[256,4,64]{2,0,1:T(8,128)(2,1)S(1)} %get-tuple-element.11), channel_id=1, source_target_pairs={{0,8},{1,9},{2,10},{3,11},{4,12},{5,13},{6,14},{7,15},{16,24},{17,... | collective-permute-start | bytes 393224 | tf_op jit(solution)/shard_map/ppermute | solution.py:17
  126.5 8.7 %collective-permute-start.3 = (bf16[256,4,64]{2,0,1:T(8,128)(2,1)S(1)}, bf16[256,4,64]{2,0,1:T(8,128)(2,1)S(1)}, u32[]{:S(2)}, u32[]{:S(2)}) collective-permute-start(bf16[256,4,64]{2,0,1:T(8,128)(2,1)S(1)} %get-tuple-element.12), channel_id=1, source_target_pairs={{8,0},{9,1},{10,2},{11,3},{12,4},{13,5},{14,6},{15,7},{24,16},{25,... | collective-permute-start | bytes 393224 | tf_op jit(solution)/shard_map/ppermute | solution.py:19
  154.3 0.9 copy-start.6
  155.2 1.2 copy-start.7
  155.2 1.2 copy-start.8
  155.2 3.5 copy-start.1
Sparse Core Ops, SparseCore 0:
  155.3 310.4 all-reduce.7
where the time goes:
time: 476 us; the launch traced here: 475 us
  waiting for transfers between devices  309 us (65%)
  blocking collectives  76.2 us (16%)
  matrix products  37.3 us (8%)
  starting transfers between devices  24.4 us (5%)
  between operations  15.2 us (3%)
  local copies, waits for them, and re-layouts  8.96 us (2%)
    psum x1, waiting for transfers between devices, shards(): summed = lax.psum(local_grad, ('gz', 'gy'))  305 us
    unnamed x1, blocking collectives  58.5 us
    dot_general x54, matrix products, apply_taps(): jnp.einsum(form, tap_weight(tz, ty, tx), piece, preferred_element_type=jn...  28.2 us
    all_gather x1, blocking collectives, shards(): whole = lax.all_gather(features, 'af', axis=0, tiled=True)  17.7 us
    ppermute x4, starting transfers between devices, extended(): lax.ppermute(tail, axis, [(i, (i + 1) % count) for i in range(ends)])  12.5 us
    ppermute x4, starting transfers between devices, extended(): lax.ppermute(head, axis, [((i + 1) % count, i) for i in range(ends)])  11.9 us
  transfers between devices with their start and end apart: 9, of which 4 were waited for; matrix products, arithmetic and copies ran while one was open for 5% of the time, Pallas kernels for 0%

commit v1 on v0

v1 whole, which is shorter than its diff:
```python
import math

import jax
import jax.numpy as jnp
from jax import lax
from jax.experimental import pallas as pl
from jax.experimental.pallas import tpu as pltpu
from jax.sharding import PartitionSpec as P

MESH = pl.DeviceIdType.MESH
F32 = jnp.float32
BF16 = jnp.bfloat16
WIDTH = 64
PLANE = 512
CELLS = 1024
OWN = 32
C = 256
TAPS = 27
ROWS = TAPS * OWN
CHUNK = ROWS // 4
SPLIT = 112
N_COPIES = 96


def tap_index(a, b, c):
    return ((a + 1) * 3 + (b + 1)) * 3 + (c + 1)


def roll(x, shift):
    return pltpu.roll(x, shift % x.shape[1], 1)


def aligned(start, size, unit):
    return pl.ds(pl.multiple_of(start, unit), size)


class Ring:
    def __init__(self, send, chunk, rows, split, pos, nxt, prv, first, from_prv, from_nxt):
        self.send, self.chunk, self.rows, self.split = send, chunk, rows, split
        self.pos, self.nxt, self.prv = pos, nxt, prv
        self.first, self.from_prv, self.from_nxt = first, from_prv, from_nxt

    def start(self):
        low, high = self.split, self.rows - self.split
        far, up, down = ((self.pos + k) % 4 for k in (2, 1, 3))
        self.far_low = self.send(self.chunk(far, 0, low), self.first.at[pl.ds(0, low)], self.nxt)
        self.far_high = self.send(self.chunk(far, low, high), self.first.at[pl.ds(low, high)], self.prv)
        self.up_high = self.send(self.chunk(up, low, high), self.from_prv.at[pl.ds(low, high)], self.nxt)
        self.down_low = self.send(self.chunk(down, 0, low), self.from_nxt.at[pl.ds(0, low)], self.prv)

    def middle(self):
        low, high = self.split, self.rows - self.split
        up, down = ((self.pos + k) % 4 for k in (1, 3))
        part = self.chunk(up, 0, low)
        self.far_low.wait_recv()
        part[...] += self.first[pl.ds(0, low)]
        self.up_low = self.send(part, self.from_prv.at[pl.ds(0, low)], self.nxt)
        part = self.chunk(down, low, high)
        self.far_high.wait_recv()
        part[...] += self.first[pl.ds(low, high)]
        self.down_high = self.send(part, self.from_nxt.at[pl.ds(low, high)], self.prv)

    def end(self):
        for copy in (self.up_high, self.down_low, self.up_low, self.down_high):
            copy.wait_recv()
        return self.chunk(self.pos, 0, self.rows)[...] + self.from_prv[...] + self.from_nxt[...]


def kernel(
    feat, cot, taps, resp_out, back_out, grad_out,
    field, cot_plane, cot_row, cim,
    back, back_in, back_sum, back_first, back_prv, back_nxt,
    z, core_sum, row_sum, core_in, row_in, row_far_in,
    grad, grad_first, grad_prv, grad_nxt, part, part_in, whole,
    send_sem, recv_sem,
):
    gz = lax.axis_index("gz")
    gy = lax.axis_index("gy")
    af = lax.axis_index("af")
    py, px = gz // 4, gz % 4
    zh, core = af // 2, af % 2

    sibling = (gz, gy, zh * 2 + (1 - core))
    z_next = (gz, gy, ((zh + 1) % 4) * 2 + core)
    z_prev = (gz, gy, ((zh + 3) % 4) * 2 + core)
    d_next, d_prev = (gz + 1) % 16, (gz + 15) % 16
    side = 1 - gy

    def along_x(k, row=gy):
        return (py * 4 + (px + k) % 4, row, af)

    def along_y(k, row=gy):
        return (((py + k) % 4) * 4 + px, row, af)

    started = []

    def send(src, dst, device):
        index = len(started)
        copy = pltpu.make_async_remote_copy(
            src_ref=src, dst_ref=dst, send_sem=send_sem.at[index], recv_sem=recv_sem.at[index],
            device_id=device, device_id_type=MESH,
        )
        copy.start()
        started.append(copy)
        return copy

    partners = [sibling, z_next, z_prev, (d_next, gy, af), (d_prev, gy, af)]
    partners += [(d_next, side, af), (d_prev, side, af), (gz, side, af)]
    for k in (1, 2, 3):
        for along in (along_x, along_y):
            partners += [along(k), along(k, side)]
    barrier = pltpu.get_barrier_semaphore()
    for partner in partners:
        pl.semaphore_signal(barrier, inc=1, device_id=partner, device_id_type=MESH)
    pl.semaphore_wait(barrier, len(partners))

    edge = (1 - gy) * (PLANE - 128)
    low_edge = cot.at[:, aligned(edge, 128, 128)]
    high_edge = cot.at[:, aligned(edge + PLANE, 128, 128)]
    halo = [
        send(cot.at[:, pl.ds(0, PLANE)], cot_plane.at[1], (d_prev, gy, af)),
        send(cot.at[:, pl.ds(PLANE, PLANE)], cot_plane.at[0], (d_next, gy, af)),
        send(low_edge, cot_row.at[1], (gz, side, af)),
        send(high_edge, cot_row.at[2], (gz, side, af)),
        send(low_edge, cot_row.at[3], (d_prev, side, af)),
        send(high_edge, cot_row.at[0], (d_next, side, af)),
    ]

    def block(channels_of, start, count):
        return field.at[aligned(channels_of * OWN + start, count, 16)]

    to_sibling = [send(feat, block(af, 0, OWN), sibling)]
    up_low = send(feat.at[pl.ds(0, 16)], block(af, 0, 16), z_next)
    down_high = send(feat.at[pl.ds(16, 16)], block(af, 16, 16), z_prev)
    up_high = send(feat.at[pl.ds(16, 16)], block(af, 16, 16), z_next)
    down_low = send(feat.at[pl.ds(0, 16)], block(af, 0, 16), z_prev)
    block(af, 0, OWN)[...] = feat[...]

    for copy in halo:
        copy.wait_recv()
    lane = lax.broadcasted_iota(jnp.int32, (OWN, PLANE + 128), 1)
    column = lane % WIDTH
    slab_lane = lax.broadcasted_iota(jnp.int32, (OWN, 128), 1)
    row_side = (slab_lane < WIDTH) == (gy == 0)
    inside = (gz > 0, None, None, gz < 15)
    for e in range(4):
        if e in (1, 2):
            plane = cot[:, pl.ds((e - 1) * PLANE, PLANE)].astype(F32)
        else:
            plane = cot_plane[e // 3].astype(F32)
        rows = jnp.where(row_side, cot_row[e].astype(F32), 0.0)
        base = jnp.concatenate([plane, rows], axis=1)
        if inside[e] is not None:
            base = jnp.where(inside[e], base, 0.0)
        for c in (-1, 0, 1):
            if c == 0:
                moved = base
            else:
                moved = jnp.where(column == (0 if c == 1 else WIDTH - 1), 0.0, roll(base, c))
            tall = roll(moved, WIDTH).astype(BF16)
            moved = moved.astype(BF16)
            for a in (-1, 0, 1):
                d = e - 1 + a
                if d not in (0, 1):
                    continue
                for b in (-1, 0, 1):
                    piece = {-1: tall[:, 128:], 0: moved[:, :PLANE], 1: tall[:, :PLANE]}[b]
                    cim[pl.ds(tap_index(a, b, c) * OWN, OWN), pl.ds(d * PLANE, PLANE)] = piece

    below, above = ((zh + 3) % 4) * 2 + core, ((zh + 1) % 4) * 2 + core
    up_low.wait_recv()
    far_low = send(block(below, 0, 16), block(below, 0, 16), z_next)
    down_high.wait_recv()
    far_high = send(block(above, 16, 16), block(above, 16, 16), z_prev)
    up_high.wait_recv()
    to_sibling.append(send(block(below, 0, OWN), block(below, 0, OWN), sibling))
    down_low.wait_recv()
    to_sibling.append(send(block(above, 0, OWN), block(above, 0, OWN), sibling))

    @pl.loop(0, 4)
    def _(n):
        cols = aligned(n * 256, 256, 256)
        back[:, cols] = lax.dot_general(
            taps[...], cim[:, cols], (((0,), (0,)), ((), ())), preferred_element_type=F32
        )

    back_copies = [
        send(back.at[aligned((2 * k + 1 - core) * OWN, OWN, OWN)], back_in.at[k], sibling)
        for k in range(4)
    ]
    far_low.wait_recv()
    far_high.wait_recv()
    far = ((zh + 2) % 4) * 2 + core
    to_sibling.append(send(block(far, 0, OWN), block(far, 0, OWN), sibling))
    for copy in to_sibling:
        copy.wait_recv()

    @pl.loop(0, 3)
    def _(n):
        rows = aligned(n * 288, 288, 288)
        product = lax.dot_general(
            cim[rows], field[...], (((1,), (1,)), ((), ())), preferred_element_type=F32
        )
        grad[0, rows] = product[:, :128]
        grad[1, rows] = product[:, 128:]

    rings = []
    for half, (pos, along) in enumerate(((px, along_x), (py, along_y))):
        def chunk(i, start, count, half=half):
            return grad.at[half, aligned(i * CHUNK + start, count, 8)]

        ring = Ring(
            send, chunk, CHUNK, SPLIT, pos, along(1), along(3),
            grad_first.at[half], grad_prv.at[half], grad_nxt.at[half],
        )
        ring.start()
        rings.append(ring)

    for k in range(4):
        back_copies[k].wait_recv()
        back_sum[k] = back[aligned((2 * k + core) * OWN, OWN, OWN)] + back_in[k]

    back_ring = Ring(
        send, lambda i, start, count: back_sum.at[i, pl.ds(start, count)], OWN, 16, zh, z_next, z_prev,
        back_first, back_prv, back_nxt,
    )
    back_ring.start()

    @pl.loop(0, 4)
    def _(n):
        cols = aligned(n * 256, 256, 256)
        z[:, cols] = jnp.dot(taps[...], field[:, cols], preferred_element_type=F32)

    for ring in rings:
        ring.middle()

    plane_lane = lane[:, :PLANE]
    plane_column = column[:, :PLANE]
    for e in range(4):
        rows_of = []
        for b in (-1, 0, 1):
            total = None
            for c in (-1, 0, 1):
                term = None
                for a in (-1, 0, 1):
                    d = e - 1 + a
                    if d in (0, 1):
                        value = z[pl.ds(tap_index(a, b, c) * OWN, OWN), pl.ds(d * PLANE, PLANE)]
                        term = value if term is None else term + value
                if c:
                    out = WIDTH - 1 if c == 1 else 0
                    term = jnp.where(plane_column == out, 0.0, roll(term, -c))
                total = term if total is None else total + term
            rows_of.append(roll(total, -b * WIDTH) if b else total)
        before, centre, after = rows_of
        core_sum[e] = (
            centre
            + jnp.where(plane_lane < PLANE - WIDTH, after, 0.0)
            + jnp.where(plane_lane >= WIDTH, before, 0.0)
        )
        outward = jnp.where(gy == 0, before[:, :128], after[:, PLANE - 128:])
        row_sum[e] = jnp.where(row_side, outward, 0.0)

    resp_copies = [
        send(core_sum.at[0], core_in.at[1], (d_prev, gy, af)),
        send(core_sum.at[3], core_in.at[0], (d_next, gy, af)),
        send(row_sum.at[1], row_in.at[0], (gz, side, af)),
        send(row_sum.at[2], row_in.at[1], (gz, side, af)),
        send(row_sum.at[0], row_far_in.at[1], (d_prev, side, af)),
        send(row_sum.at[3], row_far_in.at[0], (d_next, side, af)),
    ]
    back_ring.middle()

    groups = []
    for half, (pos, along) in enumerate(((py, along_y), (px, along_x))):
        part[half, pl.ds(0, CHUNK)] = rings[half].end()
        part[half, pl.ds(CHUNK, 256 - CHUNK)] = jnp.zeros((256 - CHUNK, 128), F32)
        mine = pos * 2 + gy
        others = []
        for step in range(1, 8):
            k, other = step // 2, gy if step % 2 == 0 else side
            there = ((pos + k) % 4) * 2 + other
            others.append((along(k, other), there))
        groups.append((mine, others))

    part_copies = []
    for half, (mine, others) in enumerate(groups):
        part_copies.append([
            send(part.at[half, aligned(there * 32, 32, 32)], part_in.at[half, n], device)
            for n, (device, there) in enumerate(others)
        ])
    scale = 1.0 / math.sqrt(32768.0)
    whole_copies = []
    for half, (mine, others) in enumerate(groups):
        rows = aligned(mine * 32, 32, 32)
        total = part[half, rows]
        for n, copy in enumerate(part_copies[half]):
            copy.wait_recv()
            total = total + part_in[half, n]
        whole[half, rows] = total * scale
        for device, _ in others:
            whole_copies.append(send(whole.at[half, rows], whole.at[half, rows], device))

    for copy in resp_copies:
        copy.wait_recv()
    for d, valid in ((0, gz > 0), (1, gz < 15)):
        total = core_sum[d + 1] + jnp.where(valid, core_in[d], 0.0)
        slab = row_in[d] + jnp.where(valid, row_far_in[d], 0.0)
        slab = jnp.concatenate(
            [
                jnp.where(gy == 1, slab, 0.0),
                jnp.zeros((OWN, PLANE - 256), F32),
                jnp.where(gy == 0, slab, 0.0),
            ],
            axis=1,
        )
        resp_out[:, pl.ds(d * PLANE, PLANE)] = (total + slab).astype(BF16)

    for copy in whole_copies:
        copy.wait_recv()
    final = []
    for half, (pos, along) in enumerate(((px, along_x), (py, along_y))):
        def place(i, start, count, half=half):
            return grad_out.at[aligned(i * CHUNK + start, count, 8), pl.ds(half * 128, 128)]

        low, high = (0, SPLIT), (SPLIT, CHUNK - SPLIT)
        nxt, prv = along(1), along(3)
        copies = []
        for device, (start, count) in ((nxt, low), (prv, high), (nxt, high), (prv, low)):
            copies.append(send(whole.at[half, pl.ds(start, count)], place(pos, start, count), device))
        place(pos, 0, CHUNK)[...] = whole[half, pl.ds(0, CHUNK)]
        final.append((copies, place, pos, nxt, prv, low, high))

    back_out[...] = back_ring.end().astype(BF16)

    last = []
    for copies, place, pos, nxt, prv, low, high in final:
        down, up = (pos + 3) % 4, (pos + 1) % 4
        copies[0].wait_recv()
        last.append(send(place(down, *low), place(down, *low), nxt))
        copies[1].wait_recv()
        last.append(send(place(up, *high), place(up, *high), prv))
        copies[2].wait_recv()
        copies[3].wait_recv()
    for copy in last:
        copy.wait_recv()
    for copy in started:
        copy.wait_send()


def shards(features, filters, cotangent):
    vmem = pl.BlockSpec(memory_space=pltpu.VMEM)
    resp, back, grad = pl.pallas_call(
        kernel,
        out_shape=(
            jax.ShapeDtypeStruct((OWN, CELLS), BF16),
            jax.ShapeDtypeStruct((OWN, CELLS), BF16),
            jax.ShapeDtypeStruct((ROWS, C), F32),
        ),
        in_specs=[vmem] * 3,
        out_specs=(vmem,) * 3,
        scratch_shapes=[
            pltpu.VMEM((C, CELLS), BF16),
            pltpu.VMEM((2, OWN, PLANE), BF16),
            pltpu.VMEM((4, OWN, 128), BF16),
            pltpu.VMEM((ROWS, CELLS), BF16),
            pltpu.VMEM((C, CELLS), F32),
            pltpu.VMEM((4, OWN, CELLS), F32),
            pltpu.VMEM((4, OWN, CELLS), F32),
            pltpu.VMEM((OWN, CELLS), F32),
            pltpu.VMEM((OWN, CELLS), F32),
            pltpu.VMEM((OWN, CELLS), F32),
            pltpu.VMEM((ROWS, CELLS), F32),
            pltpu.VMEM((4, OWN, PLANE), F32),
            pltpu.VMEM((4, OWN, 128), F32),
            pltpu.VMEM((2, OWN, PLANE), F32),
            pltpu.VMEM((2, OWN, 128), F32),
            pltpu.VMEM((2, OWN, 128), F32),
            pltpu.VMEM((2, ROWS, 128), F32),
            pltpu.VMEM((2, CHUNK, 128), F32),
            pltpu.VMEM((2, CHUNK, 128), F32),
            pltpu.VMEM((2, CHUNK, 128), F32),
            pltpu.VMEM((2, 256, 128), F32),
            pltpu.VMEM((2, 7, 32, 128), F32),
            pltpu.VMEM((2, 256, 128), F32),
            pltpu.SemaphoreType.DMA((N_COPIES,)),
            pltpu.SemaphoreType.DMA((N_COPIES,)),
        ],
        compiler_params=pltpu.CompilerParams(
            collective_id=0, has_side_effects=True, vmem_limit_bytes=40 * 1024 * 1024
        ),
    )(
        features.reshape(OWN, CELLS),
        cotangent.reshape(OWN, CELLS),
        filters.reshape(ROWS, C),
    )
    return (
        resp.reshape(features.shape),
        back.reshape(cotangent.shape),
        grad.reshape(filters.shape),
    )


def solution(mesh):
    placed = (P("af", "gz", "gy"), P(None, None, None, "af", None), P("af", "gz", "gy"))
    return jax.shard_map(
        shards,
        mesh=mesh,
        in_specs=placed,
        out_specs=(P("af", "gz", "gy"), P("af", "gz", "gy"), P(None, None, None, "af", None)),
        check_vma=False,
    )
```

time: 476 us -> 57 us (0.12)
  the two profiles are of different devices: /device:TPU:32 before, /device:TPU:1 now
where the time goes in v1:
time: 57 us; the launch traced here: 55.9 us
  Pallas kernels  51.1 us (90%)
  local copies, waits for them, and re-layouts  4.14 us (7%)
  between operations  0.67 us (1%)
    pallas_call x1, Pallas kernels, shards(): pl.pallas_call(kernel, out_shape=(jax.ShapeDtypeStruct((OWN, CELLS), BF16...  51.1 us
    unnamed x7, local copies, waits for them, and re-layouts  2.81 us

profile of v1, /device:TPU:1, one launch (start us, length us, event | category | flops | bytes accessed | tf_op | source)
XLA Modules:
  0.0 55.9 jit_solution(15351913713714930496)
XLA Ops:
  0.6 0.0 copy-start.1
  0.6 0.9 %copy.6 = bf16[4,8,2,512]{3,1,2,0:T(8,128)(2,1)S(1)} copy(bf16[4,8,2,512]{3,2,1,0:T(2,128)(2,1)} %bitcast.10) | data formatting | bytes 131072
  1.5 0.0 copy-done.1
  1.6 0.0 copy-start
  1.6 1.0 %copy-done = bf16[3,3,3,32,256]{4,3,2,1,0:T(8,128)(2,1)S(1)} copy-done((bf16[3,3,3,32,256]{4,3,2,1,0:T(8,128)(2,1)S(1)}, bf16[3,3,3,32,256]{4,3,2,1,0:T(8,128)(2,1)}, u32[]{:S(2)}) %copy-start) | copy-done | bytes 442392
  2.6 51.1 %shard_map.58 = (bf16[32,1024]{1,0:T(8,128)(2,1)S(1)}, bf16[32,1024]{1,0:T(8,128)(2,1)S(1)}, f32[864,256]{1,0:T(8,128)S(1)}) custom-call(bf16[32,1024]{1,0:T(8,128)(2,1)S(1)} %bitcast.8, bf16[32,1024]{1,0:T(8,128)(2,1)S(1)} %bitcast.9, bf16[864,256]{1,0:T(8,128)(2,1)S(1)} %bitcast.7), custom_call_target="tpu_custom_call" | custom-call | tf_op jit(solution)/shard_map/pallas_call | solution.py:353
  53.6 0.7 %reshape.27 = bf16[32,2,512]{2,1,0:T(2,128)(2,1)} reshape(bf16[32,1024]{1,0:T(8,128)(2,1)S(1)} %get-tuple-element.6) | data formatting | bytes 131072 | tf_op jit(solution)/shard_map/reshape | solution.py:398
  54.3 0.7 %reshape.28 = bf16[32,2,512]{2,1,0:T(2,128)(2,1)} reshape(bf16[32,1024]{1,0:T(8,128)(2,1)S(1)} %get-tuple-element.7) | data formatting | bytes 131072 | tf_op jit(solution)/shard_map/reshape | solution.py:399
  55.0 0.9 %copy.9 = f32[3,3,3,32,256]{4,3,2,1,0:T(8,128)} copy(f32[3,3,3,32,256]{4,3,2,1,0:T(8,128)S(1)} %bitcast.6) | data formatting | bytes 1769472
  (1 shorter events, 0.0 us)
Async XLA Ops:
  0.6 0.9 %copy-start.1 = (bf16[32,2,512]{2,1,0:T(2,128)(2,1)S(1)}, bf16[32,2,512]{2,1,0:T(2,128)(2,1)}, u32[]{:S(2)}) copy-start(bf16[32,2,512]{2,1,0:T(2,128)(2,1)} %param.5) | copy-start | bytes 196612
  1.6 1.0 %copy-start = (bf16[3,3,3,32,256]{4,3,2,1,0:T(8,128)(2,1)S(1)}, bf16[3,3,3,32,256]{4,3,2,1,0:T(8,128)(2,1)}, u32[]{:S(2)}) copy-start(bf16[3,3,3,32,256]{4,3,2,1,0:T(8,128)(2,1)} %param.4) | copy-start | bytes 1327108

commit v2 on v1

v2 whole, which is shorter than its diff:
```python
import math

import jax
import jax.numpy as jnp
from jax import lax
from jax.experimental import pallas as pl
from jax.experimental.pallas import tpu as pltpu
from jax.sharding import PartitionSpec as P

MESH = pl.DeviceIdType.MESH
F32 = jnp.float32
BF16 = jnp.bfloat16
WIDTH = 64
PLANE = 512
CELLS = 1024
OWN = 32
C = 256
TAPS = 27
ROWS = TAPS * OWN
PADDED = 896
CHUNK = PADDED // 8
N_GROUPS = 32


def tap_index(a, b, c):
    return ((a + 1) * 3 + (b + 1)) * 3 + (c + 1)


def roll(x, shift):
    return pltpu.roll(x, shift % x.shape[1], 1)


def aligned(start, size, unit):
    return pl.ds(pl.multiple_of(start, unit), size)


class Ring:
    def __init__(self, group, chunk, rows, split, pos, nxt, prv, first, both):
        self.group, self.chunk, self.rows, self.split = group, chunk, rows, split
        self.pos, self.nxt, self.prv = pos, nxt, prv
        self.first, self.both = first, both

    def start(self):
        low, high = self.split, self.rows - self.split
        far, up, down = ((self.pos + k) % 4 for k in (2, 1, 3))
        self.early = self.group(self.first)
        self.early.send(self.chunk(far, 0, low), self.first.at[pl.ds(0, low)], self.nxt)
        self.early.send(self.chunk(far, low, high), self.first.at[pl.ds(low, high)], self.prv)
        self.late = self.group(self.both)
        self.late.send(self.chunk(up, low, high), self.both.at[0, pl.ds(low, high)], self.nxt)
        self.late.send(self.chunk(down, 0, low), self.both.at[1, pl.ds(0, low)], self.prv)

    def middle(self):
        low, high = self.split, self.rows - self.split
        up, down = ((self.pos + k) % 4 for k in (1, 3))
        self.early.wait_recv()
        part = self.chunk(up, 0, low)
        part[...] += self.first[pl.ds(0, low)]
        self.late.send(part, self.both.at[0, pl.ds(0, low)], self.nxt)
        part = self.chunk(down, low, high)
        part[...] += self.first[pl.ds(low, high)]
        self.late.send(part, self.both.at[1, pl.ds(low, high)], self.prv)

    def end(self):
        self.late.wait_recv()
        return self.chunk(self.pos, 0, self.rows)[...] + self.both[0] + self.both[1]


def kernel(
    feat, cot, taps, resp_out, back_out, grad_out,
    field, cot_halo, cim,
    back, back_in, back_sum, back_first, back_both,
    z, core_sum, row_sum, resp_in,
    grad, grad_in, part, part_in, whole,
    send_sem, recv_sem,
):
    gz = lax.axis_index("gz")
    gy = lax.axis_index("gy")
    af = lax.axis_index("af")
    py, px = gz // 4, gz % 4
    zh, core = af // 2, af % 2

    sibling = (gz, gy, zh * 2 + (1 - core))
    d_next, d_prev = (gz + 1) % 16, (gz + 15) % 16
    side = 1 - gy

    def along_x(k, row=gy):
        return (py * 4 + (px + k) % 4, row, af)

    def along_y(k, row=gy):
        return (((py + k) % 4) * 4 + px, row, af)

    def along_z(k):
        return (gz, gy, ((zh + k) % 4) * 2 + core)

    groups = []

    class Group:
        def __init__(self, size):
            self.index, self.size = len(groups), size
            groups.append(self)

        def send(self, src, dst, device):
            pltpu.make_async_remote_copy(
                src_ref=src, dst_ref=dst,
                send_sem=send_sem.at[self.index], recv_sem=recv_sem.at[self.index],
                device_id=device, device_id_type=MESH,
            ).start()
            return self

        def wait_recv(self):
            pltpu.make_async_copy(self.size, self.size, recv_sem.at[self.index]).wait()

        def wait_send(self):
            pltpu.make_async_copy(self.size, self.size, send_sem.at[self.index]).wait()

    partners = [sibling, (d_next, gy, af), (d_prev, gy, af)]
    partners += [(d_next, side, af), (d_prev, side, af), (gz, side, af)]
    for k in (1, 2, 3):
        partners.append(along_z(k))
        for along in (along_x, along_y):
            partners += [along(k), along(k, side)]
    barrier = pltpu.get_barrier_semaphore()
    for partner in partners:
        pl.semaphore_signal(barrier, inc=1, device_id=partner, device_id_type=MESH)
    pl.semaphore_wait(barrier, len(partners))

    def block(channels_of):
        return field.at[aligned(channels_of * OWN, OWN, OWN)]

    def relay(k):
        rows = block(((zh + k) % 4) * 2 + core)
        return Group(rows).send(rows, rows, sibling)

    pair = 1 + 2 * (zh % 2)
    from_pair = Group(block(af)).send(feat, block(af), along_z(pair))
    from_sibling = Group(block(af)).send(feat, block(af), sibling)

    edge = (1 - gy) * (PLANE - 128)
    low_edge = cot.at[:, aligned(edge, 128, 128)]
    high_edge = cot.at[:, aligned(edge + PLANE, 128, 128)]

    def halo(n):
        return cot_halo.at[:, pl.ds(2 * PLANE + n * 128, 128)]

    halos = Group(cot_halo)
    halos.send(low_edge, halo(3), (d_prev, side, af))
    halos.send(high_edge, halo(0), (d_next, side, af))
    halos.send(cot.at[:, pl.ds(0, PLANE)], cot_halo.at[:, pl.ds(PLANE, PLANE)], (d_prev, gy, af))
    halos.send(cot.at[:, pl.ds(PLANE, PLANE)], cot_halo.at[:, pl.ds(0, PLANE)], (d_next, gy, af))
    halos.send(low_edge, halo(1), (gz, side, af))
    halos.send(high_edge, halo(2), (gz, side, af))
    from_far = Group(block(af)).send(feat, block(af), along_z(2))
    from_other = Group(block(af)).send(feat, block(af), along_z(4 - pair))
    block(af)[...] = feat[...]

    from_pair.wait_recv()
    pair_relay = relay(pair)

    halos.wait_recv()
    lane = lax.broadcasted_iota(jnp.int32, (OWN, PLANE + 128), 1)
    column = lane % WIDTH
    slab_lane = lax.broadcasted_iota(jnp.int32, (OWN, 128), 1)
    row_side = (slab_lane < WIDTH) == (gy == 0)
    inside = (gz > 0, None, None, gz < 15)
    for e in range(4):
        if e in (1, 2):
            plane = cot[:, pl.ds((e - 1) * PLANE, PLANE)].astype(F32)
        else:
            plane = cot_halo[:, pl.ds((e // 3) * PLANE, PLANE)].astype(F32)
        rows = jnp.where(row_side, halo(e)[...].astype(F32), 0.0)
        base = jnp.concatenate([plane, rows], axis=1)
        if inside[e] is not None:
            base = jnp.where(inside[e], base, 0.0)
        for c in (-1, 0, 1):
            if c == 0:
                moved = base
            else:
                moved = jnp.where(column == (0 if c == 1 else WIDTH - 1), 0.0, roll(base, c))
            tall = roll(moved, WIDTH).astype(BF16)
            moved = moved.astype(BF16)
            for a in (-1, 0, 1):
                d = e - 1 + a
                if d not in (0, 1):
                    continue
                for b in (-1, 0, 1):
                    piece = {-1: tall[:, 128:], 0: moved[:, :PLANE], 1: tall[:, :PLANE]}[b]
                    cim[pl.ds(tap_index(a, b, c) * OWN, OWN), pl.ds(d * PLANE, PLANE)] = piece

    near_lanes = (zh // 2) * 128

    def channels(half):
        return near_lanes if half == 0 else 128 - near_lanes

    def filter_products(half):
        @pl.loop(0, 3)
        def _(n):
            rows = aligned(n * 288, 288, 288)
            grad[half, rows] = lax.dot_general(
                cim[rows], field[aligned(channels(half), 128, 128)],
                (((1,), (1,)), ((), ())), preferred_element_type=F32,
            )
        grad[half, pl.ds(ROWS, PADDED - ROWS)] = jnp.zeros((PADDED - ROWS, 128), F32)

    orders = ((px, along_x, py, along_y), (py, along_y, px, along_x))

    def unit_rows(r, i):
        return aligned(r * 4 * CHUNK + i * CHUNK, CHUNK, 16)

    def scatter(half):
        for r, (pos, along, _, _) in enumerate(orders):
            u = half * 2 + r
            sent = Group(grad_in.at[u])
            for k in (2, 1, 3):
                sent.send(grad.at[half, unit_rows(r, (pos + k) % 4)], grad_in.at[u, k - 1], along(k))
            scattered[u] = sent

    def eight(pos, along):
        others = []
        for step in (5, 4, 3, 2, 7, 6, 1):
            k, row = step // 2, gy if step % 2 == 0 else side
            others.append((step - 1, along(k, row), ((pos + k) % 4) * 2 + row))
        return pos * 2 + gy, others

    def scatter_again(half):
        for r, (pos, _, pos2, along2) in enumerate(orders):
            u = half * 2 + r
            scattered[u].wait_recv()
            part[u, pl.ds(0, CHUNK)] = (
                grad[half, unit_rows(r, pos)] + grad_in[u, 0] + grad_in[u, 1] + grad_in[u, 2]
            )
            part[u, pl.ds(CHUNK, 16)] = jnp.zeros((16, 128), F32)
            sent = Group(part_in.at[u])
            for n, device, there in eight(pos2, along2)[1]:
                sent.send(part.at[u, aligned(there * 16, 16, 16)], part_in.at[u, n], device)
            scattered_again[u] = sent

    def gather(half):
        for r, (_, _, pos2, along2) in enumerate(orders):
            u = half * 2 + r
            mine, others = eight(pos2, along2)
            rows = aligned(mine * 16, 16, 16)
            scattered_again[u].wait_recv()
            total = part[u, rows]
            for n in range(7):
                total = total + part_in[u, n]
            whole[u, rows] = total * (1.0 / math.sqrt(32768.0))
            sent = Group(part_in.at[u])
            for _, device, _ in others:
                sent.send(whole.at[u, rows], whole.at[u, rows], device)
            gathered[u] = sent

    def gather_again(half):
        lanes = aligned(channels(half), 128, 128)
        for r, (pos, along, _, _) in enumerate(orders):
            u = half * 2 + r
            gathered[u].wait_recv()
            sent = Group(grad_in.at[u])
            place = grad_out.at[unit_rows(r, pos), lanes]
            for k in (2, 1, 3):
                sent.send(whole.at[u, pl.ds(0, CHUNK)], place, along(k))
            place[...] = whole[u, pl.ds(0, CHUNK)]
            gathered_again[u] = sent

    scattered, scattered_again, gathered, gathered_again = {}, {}, {}, {}

    from_sibling.wait_recv()
    pair_relay.wait_recv()
    filter_products(0)
    scatter(0)
    from_other.wait_recv()
    other_relay = relay(4 - pair)

    @pl.loop(0, 4)
    def _(n):
        cols = aligned(n * 256, 256, 256)
        back[:, cols] = lax.dot_general(
            taps[...], cim[:, cols], (((0,), (0,)), ((), ())), preferred_element_type=F32
        )

    from_far.wait_recv()
    far_relay = relay(2)
    to_sibling = Group(back_in)
    for k in range(4):
        to_sibling.send(back.at[aligned((2 * k + 1 - core) * OWN, OWN, OWN)], back_in.at[k], sibling)
    other_relay.wait_recv()
    far_relay.wait_recv()
    filter_products(1)
    scatter(1)

    to_sibling.wait_recv()
    for k in range(4):
        back_sum[k] = back[aligned((2 * k + core) * OWN, OWN, OWN)] + back_in[k]

    ring = Ring(
        Group, lambda i, start, count: back_sum.at[i, pl.ds(start, count)], OWN, 16,
        zh, along_z(1), along_z(3), back_first, back_both,
    )
    ring.start()

    @pl.loop(0, 4)
    def _(n):
        cols = aligned(n * 256, 256, 256)
        z[:, cols] = jnp.dot(taps[...], field[:, cols], preferred_element_type=F32)

    scatter_again(0)

    plane_lane = lane[:, :PLANE]
    plane_column = column[:, :PLANE]
    for e in range(4):
        rows_of = []
        for b in (-1, 0, 1):
            total = None
            for c in (-1, 0, 1):
                term = None
                for a in (-1, 0, 1):
                    d = e - 1 + a
                    if d in (0, 1):
                        value = z[pl.ds(tap_index(a, b, c) * OWN, OWN), pl.ds(d * PLANE, PLANE)]
                        term = value if term is None else term + value
                if c:
                    out = WIDTH - 1 if c == 1 else 0
                    term = jnp.where(plane_column == out, 0.0, roll(term, -c))
                total = term if total is None else total + term
            rows_of.append(roll(total, -b * WIDTH) if b else total)
        before, centre, after = rows_of
        core_sum[e] = (
            centre
            + jnp.where(plane_lane < PLANE - WIDTH, after, 0.0)
            + jnp.where(plane_lane >= WIDTH, before, 0.0)
        )
        outward = jnp.where(gy == 0, before[:, :128], after[:, PLANE - 128:])
        row_sum[e] = jnp.where(row_side, outward, 0.0)

    def resp_row(n):
        return resp_in.at[:, pl.ds(2 * PLANE + n * 128, 128)]

    outer = Group(resp_in)
    outer.send(core_sum.at[0], resp_in.at[:, pl.ds(PLANE, PLANE)], (d_prev, gy, af))
    outer.send(core_sum.at[3], resp_in.at[:, pl.ds(0, PLANE)], (d_next, gy, af))
    outer.send(row_sum.at[1], resp_row(0), (gz, side, af))
    outer.send(row_sum.at[2], resp_row(1), (gz, side, af))
    outer.send(row_sum.at[0], resp_row(3), (d_prev, side, af))
    outer.send(row_sum.at[3], resp_row(2), (d_next, side, af))

    scatter_again(1)
    ring.middle()
    gather(0)

    outer.wait_recv()
    for d, valid in ((0, gz > 0), (1, gz < 15)):
        total = core_sum[d + 1] + jnp.where(valid, resp_in[:, pl.ds(d * PLANE, PLANE)], 0.0)
        slab = resp_row(d)[...] + jnp.where(valid, resp_row(2 + d)[...], 0.0)
        slab = jnp.concatenate(
            [
                jnp.where(gy == 1, slab, 0.0),
                jnp.zeros((OWN, PLANE - 256), F32),
                jnp.where(gy == 0, slab, 0.0),
            ],
            axis=1,
        )
        resp_out[:, pl.ds(d * PLANE, PLANE)] = (total + slab).astype(BF16)

    gather(1)
    gather_again(0)
    gather_again(1)
    back_out[...] = ring.end().astype(BF16)
    for u in range(4):
        gathered_again[u].wait_recv()
    for group in groups:
        group.wait_send()


def shards(features, filters, cotangent):
    vmem = pl.BlockSpec(memory_space=pltpu.VMEM)
    resp, back, grad = pl.pallas_call(
        kernel,
        out_shape=(
            jax.ShapeDtypeStruct((OWN, CELLS), BF16),
            jax.ShapeDtypeStruct((OWN, CELLS), BF16),
            jax.ShapeDtypeStruct((PADDED, C), F32),
        ),
        in_specs=[vmem] * 3,
        out_specs=(vmem,) * 3,
        scratch_shapes=[
            pltpu.VMEM((C, CELLS), BF16),
            pltpu.VMEM((OWN, 2 * PLANE + 4 * 128), BF16),
            pltpu.VMEM((ROWS, CELLS), BF16),
            pltpu.VMEM((C, CELLS), F32),
            pltpu.VMEM((4, OWN, CELLS), F32),
            pltpu.VMEM((4, OWN, CELLS), F32),
            pltpu.VMEM((OWN, CELLS), F32),
            pltpu.VMEM((2, OWN, CELLS), F32),
            pltpu.VMEM((ROWS, CELLS), F32),
            pltpu.VMEM((4, OWN, PLANE), F32),
            pltpu.VMEM((4, OWN, 128), F32),
            pltpu.VMEM((OWN, 2 * PLANE + 4 * 128), F32),
            pltpu.VMEM((2, PADDED, 128), F32),
            pltpu.VMEM((4, 3, CHUNK, 128), F32),
            pltpu.VMEM((4, CHUNK + 16, 128), F32),
            pltpu.VMEM((4, 7, 16, 128), F32),
            pltpu.VMEM((4, CHUNK + 16, 128), F32),
            pltpu.SemaphoreType.DMA((N_GROUPS,)),
            pltpu.SemaphoreType.DMA((N_GROUPS,)),
        ],
        compiler_params=pltpu.CompilerParams(
            collective_id=0, has_side_effects=True, vmem_limit_bytes=40 * 1024 * 1024
        ),
    )(
        features.reshape(OWN, CELLS),
        cotangent.reshape(OWN, CELLS),
        filters.reshape(ROWS, C),
    )
    return (
        resp.reshape(features.shape),
        back.reshape(cotangent.shape),
        grad[:ROWS].reshape(filters.shape),
    )


def solution(mesh):
    placed = (P("af", "gz", "gy"), P(None, None, None, "af", None), P("af", "gz", "gy"))
    return jax.shard_map(
        shards,
        mesh=mesh,
        in_specs=placed,
        out_specs=(P("af", "gz", "gy"), P("af", "gz", "gy"), P(None, None, None, "af", None)),
        check_vma=False,
    )
```

time: 57 us -> 52.9 us (0.928); the launches traced: 55.9 us -> 52.7 us
  Pallas kernels: 51.1 us -> 47.8 us
    pallas_call x1, Pallas kernels: 51.1 us -> 47.8 us  [shards(): pl.pallas_call(kernel, out_shape=(jax.ShapeDtypeStruct((OWN, CELLS), BF16...]
    slice x0 -> x1, local copies, waits for them, and re-layouts: none -> 0.97 us  [shards(): grad[:ROWS].reshape(filters.shape)]
    unnamed x7 -> x6, local copies, waits for them, and re-layouts: 2.81 us -> 1.9 us
where the time goes in v2:
time: 52.9 us; the launch traced here: 52.7 us
  Pallas kernels  47.8 us (90%)
  local copies, waits for them, and re-layouts  4.19 us (8%)
  between operations  0.67 us (1%)
    pallas_call x1, Pallas kernels, shards(): pl.pallas_call(kernel, out_shape=(jax.ShapeDtypeStruct((OWN, CELLS), BF16...  47.8 us
    unnamed x6, local copies, waits for them, and re-layouts  1.9 us

profile of v2, /device:TPU:1, one launch (start us, length us, event | category | flops | bytes accessed | tf_op | source)
XLA Modules:
  0.0 52.7 jit_solution(9518886706698803769)
XLA Ops:
  0.6 0.0 copy-start.1
  0.6 0.9 %copy.6 = bf16[4,8,2,512]{3,1,2,0:T(8,128)(2,1)S(1)} copy(bf16[4,8,2,512]{3,2,1,0:T(2,128)(2,1)} %bitcast.10) | data formatting | bytes 131072
  1.5 0.0 copy-done.1
  1.6 0.0 copy-start
  1.6 1.0 %copy-done = bf16[3,3,3,32,256]{4,3,2,1,0:T(8,128)(2,1)S(1)} copy-done((bf16[3,3,3,32,256]{4,3,2,1,0:T(8,128)(2,1)S(1)}, bf16[3,3,3,32,256]{4,3,2,1,0:T(8,128)(2,1)}, u32[]{:S(2)}) %copy-start) | copy-done | bytes 442392
  2.6 47.8 %shard_map.58 = (bf16[32,1024]{1,0:T(8,128)(2,1)S(1)}, bf16[32,1024]{1,0:T(8,128)(2,1)S(1)}, f32[896,256]{1,0:T(8,128)S(1)}) custom-call(bf16[32,1024]{1,0:T(8,128)(2,1)S(1)} %bitcast.7, bf16[32,1024]{1,0:T(8,128)(2,1)S(1)} %bitcast.8, bf16[864,256]{1,0:T(8,128)(2,1)S(1)} %bitcast.6), custom_call_target="tpu_custom_call" | custom-call | tf_op jit(solution)/shard_map/pallas_call | solution.py:376
  50.4 0.7 %reshape.27 = bf16[32,2,512]{2,1,0:T(2,128)(2,1)} reshape(bf16[32,1024]{1,0:T(8,128)(2,1)S(1)} %get-tuple-element.6) | data formatting | bytes 131072 | tf_op jit(solution)/shard_map/reshape | solution.py:415
  51.1 0.7 %reshape.28 = bf16[32,2,512]{2,1,0:T(2,128)(2,1)} reshape(bf16[32,1024]{1,0:T(8,128)(2,1)S(1)} %get-tuple-element.7) | data formatting | bytes 131072 | tf_op jit(solution)/shard_map/reshape | solution.py:416
  51.7 1.0 %slice.3 = f32[864,256]{1,0:T(8,128)} slice(f32[896,256]{1,0:T(8,128)S(1)} %get-tuple-element.8), slice={[0:864], [0:256]} | slice | bytes 1769472 | tf_op jit(solution)/shard_map/slice | solution.py:417
  (1 shorter events, 0.0 us)
Async XLA Ops:
  0.6 0.9 %copy-start.1 = (bf16[32,2,512]{2,1,0:T(2,128)(2,1)S(1)}, bf16[32,2,512]{2,1,0:T(2,128)(2,1)}, u32[]{:S(2)}) copy-start(bf16[32,2,512]{2,1,0:T(2,128)(2,1)} %param.5) | copy-start | bytes 196612
  1.6 1.0 %copy-start = (bf16[3,3,3,32,256]{4,3,2,1,0:T(8,128)(2,1)S(1)}, bf16[3,3,3,32,256]{4,3,2,1,0:T(8,128)(2,1)}, u32[]{:S(2)}) copy-start(bf16[3,3,3,32,256]{4,3,2,1,0:T(8,128)(2,1)} %param.4) | copy-start | bytes 1327108

commit v3 on v2

--- a/solution.py
+++ b/solution.py
@@ -67,13 +67,19 @@
 
 
 def kernel(
-    feat, cot, taps, resp_out, back_out, grad_out,
-    field, cot_halo, cim,
+    feat_hbm, cot_hbm, taps_hbm, resp_out, back_out, grad_out,
+    feat_raw, cot_raw, taps, taps_t, feat, cot, field, cot_halo, cim,
     back, back_in, back_sum, back_first, back_both,
     z, core_sum, row_sum, resp_in,
     grad, grad_in, part, part_in, whole,
-    send_sem, recv_sem,
+    load_sem, send_sem, recv_sem,
 ):
+    loads = [
+        pltpu.make_async_copy(src, dst, load_sem.at[n])
+        for n, (src, dst) in enumerate(((feat_hbm, feat_raw), (cot_hbm, cot_raw), (taps_hbm, taps)))
+    ]
+    for load in loads:
+        load.start()
     gz = lax.axis_index("gz")
     gy = lax.axis_index("gy")
     af = lax.axis_index("af")
@@ -116,23 +122,37 @@
 
     partners = [sibling, (d_next, gy, af), (d_prev, gy, af)]
     partners += [(d_next, side, af), (d_prev, side, af), (gz, side, af)]
+    partners += [along_z(1), along_z(3)]
     for k in (1, 2, 3):
-        partners.append(along_z(k))
         for along in (along_x, along_y):
             partners += [along(k), along(k, side)]
     barrier = pltpu.get_barrier_semaphore()
     for partner in partners:
         pl.semaphore_signal(barrier, inc=1, device_id=partner, device_id_type=MESH)
+    for load, raw, flat in zip(loads, (feat_raw, cot_raw), (feat, cot)):
+        load.wait()
+        for d in (0, 1):
+            flat[:, pl.ds(d * PLANE, PLANE)] = raw[:, d, :]
+    loads[2].wait()
+    taps_t[...] = taps[...].T
     pl.semaphore_wait(barrier, len(partners))
 
     def block(channels_of):
         return field.at[aligned(channels_of * OWN, OWN, OWN)]
 
-    def relay(k):
-        rows = block(((zh + k) % 4) * 2 + core)
-        return Group(rows).send(rows, rows, sibling)
-
     pair = 1 + 2 * (zh % 2)
+    other = 4 - pair
+    far = 2
+
+    def owner(k):
+        return ((zh + k) % 4) * 2 + core
+
+    def pass_on(rows, device):
+        return Group(rows).send(rows, rows, device)
+
+    def half_block(k, start):
+        return field.at[aligned(owner(k) * OWN + start, 16, 16)]
+
     from_pair = Group(block(af)).send(feat, block(af), along_z(pair))
     from_sibling = Group(block(af)).send(feat, block(af), sibling)
 
@@ -150,12 +170,12 @@
     halos.send(cot.at[:, pl.ds(PLANE, PLANE)], cot_halo.at[:, pl.ds(0, PLANE)], (d_next, gy, af))
     halos.send(low_edge, halo(1), (gz, side, af))
     halos.send(high_edge, halo(2), (gz, side, af))
-    from_far = Group(block(af)).send(feat, block(af), along_z(2))
-    from_other = Group(block(af)).send(feat, block(af), along_z(4 - pair))
+    from_other = Group(block(af)).send(feat, block(af), along_z(other))
     block(af)[...] = feat[...]
 
     from_pair.wait_recv()
-    pair_relay = relay(pair)
+    far_by_other = pass_on(half_block(pair, 0), along_z(other))
+    pair_relay = pass_on(block(owner(pair)), sibling)
 
     halos.wait_recv()
     lane = lax.broadcasted_iota(jnp.int32, (OWN, PLANE + 128), 1)
@@ -193,13 +213,10 @@
         return near_lanes if half == 0 else 128 - near_lanes
 
     def filter_products(half):
-        @pl.loop(0, 3)
-        def _(n):
-            rows = aligned(n * 288, 288, 288)
-            grad[half, rows] = lax.dot_general(
-                cim[rows], field[aligned(channels(half), 128, 128)],
-                (((1,), (1,)), ((), ())), preferred_element_type=F32,
-            )
+        grad[half, pl.ds(0, ROWS)] = lax.dot_general(
+            cim[...], field[aligned(channels(half), 128, 128)],
+            (((1,), (1,)), ((), ())), preferred_element_type=F32,
+        )
         grad[half, pl.ds(ROWS, PADDED - ROWS)] = jnp.zeros((PADDED - ROWS, 128), F32)
 
     orders = ((px, along_x, py, along_y), (py, along_y, px, along_x))
@@ -264,22 +281,24 @@
 
     scattered, scattered_again, gathered, gathered_again = {}, {}, {}, {}
 
+    from_other.wait_recv()
+    far_by_pair = pass_on(half_block(other, 16), along_z(pair))
+    other_relay = pass_on(block(owner(other)), sibling)
     from_sibling.wait_recv()
     pair_relay.wait_recv()
     filter_products(0)
     scatter(0)
-    from_other.wait_recv()
-    other_relay = relay(4 - pair)
 
     @pl.loop(0, 4)
     def _(n):
         cols = aligned(n * 256, 256, 256)
         back[:, cols] = lax.dot_general(
-            taps[...], cim[:, cols], (((0,), (0,)), ((), ())), preferred_element_type=F32
+            taps_t[...], cim[:, cols], (((1,), (0,)), ((), ())), preferred_element_type=F32
         )
 
-    from_far.wait_recv()
-    far_relay = relay(2)
+    far_by_other.wait_recv()
+    far_by_pair.wait_recv()
+    far_relay = pass_on(block(owner(far)), sibling)
     to_sibling = Group(back_in)
     for k in range(4):
         to_sibling.send(back.at[aligned((2 * k + 1 - core) * OWN, OWN, OWN)], back_in.at[k], sibling)
@@ -288,6 +307,13 @@
     filter_products(1)
     scatter(1)
 
+    @pl.loop(0, 4)
+    def _(n):
+        cols = aligned(n * 256, 256, 256)
+        z[:, cols] = jnp.dot(taps[...], field[:, cols], preferred_element_type=F32)
+
+    scatter_again(0)
+
     to_sibling.wait_recv()
     for k in range(4):
         back_sum[k] = back[aligned((2 * k + core) * OWN, OWN, OWN)] + back_in[k]
@@ -297,13 +323,6 @@
         zh, along_z(1), along_z(3), back_first, back_both,
     )
     ring.start()
-
-    @pl.loop(0, 4)
-    def _(n):
-        cols = aligned(n * 256, 256, 256)
-        z[:, cols] = jnp.dot(taps[...], field[:, cols], preferred_element_type=F32)
-
-    scatter_again(0)
 
     plane_lane = lane[:, :PLANE]
     plane_column = column[:, :PLANE]
@@ -344,8 +363,8 @@
     outer.send(row_sum.at[3], resp_row(2), (d_next, side, af))
 
     scatter_again(1)
+    gather(0)
     ring.middle()
-    gather(0)
 
     outer.wait_recv()
     for d, valid in ((0, gz > 0), (1, gz < 15)):
@@ -359,12 +378,14 @@
             ],
             axis=1,
         )
-        resp_out[:, pl.ds(d * PLANE, PLANE)] = (total + slab).astype(BF16)
+        resp_out[:, d, :] = (total + slab).astype(BF16)
 
     gather(1)
     gather_again(0)
     gather_again(1)
-    back_out[...] = ring.end().astype(BF16)
+    total = ring.end().astype(BF16)
+    for d in (0, 1):
+        back_out[:, d, :] = total[:, d * PLANE:(d + 1) * PLANE]
     for u in range(4):
         gathered_again[u].wait_recv()
     for group in groups:
@@ -376,13 +397,19 @@
     resp, back, grad = pl.pallas_call(
         kernel,
         out_shape=(
-            jax.ShapeDtypeStruct((OWN, CELLS), BF16),
-            jax.ShapeDtypeStruct((OWN, CELLS), BF16),
+            jax.ShapeDtypeStruct((OWN, 2, PLANE), BF16),
+            jax.ShapeDtypeStruct((OWN, 2, PLANE), BF16),
             jax.ShapeDtypeStruct((PADDED, C), F32),
         ),
-        in_specs=[vmem] * 3,
+        in_specs=[pl.BlockSpec(memory_space=pl.ANY)] * 3,
         out_specs=(vmem,) * 3,
         scratch_shapes=[
+            pltpu.VMEM((OWN, 2, PLANE), BF16),
+            pltpu.VMEM((OWN, 2, PLANE), BF16),
+            pltpu.VMEM((ROWS, C), BF16),
+            pltpu.VMEM((C, ROWS), BF16),
+            pltpu.VMEM((OWN, CELLS), BF16),
+            pltpu.VMEM((OWN, CELLS), BF16),
             pltpu.VMEM((C, CELLS), BF16),
             pltpu.VMEM((OWN, 2 * PLANE + 4 * 128), BF16),
             pltpu.VMEM((ROWS, CELLS), BF16),
@@ -400,22 +427,19 @@
             pltpu.VMEM((4, CHUNK + 16, 128), F32),
             pltpu.VMEM((4, 7, 16, 128), F32),
             pltpu.VMEM((4, CHUNK + 16, 128), F32),
+            pltpu.SemaphoreType.DMA((3,)),
             pltpu.SemaphoreType.DMA((N_GROUPS,)),
             pltpu.SemaphoreType.DMA((N_GROUPS,)),
         ],
         compiler_params=pltpu.CompilerParams(
-            collective_id=0, has_side_effects=True, vmem_limit_bytes=40 * 1024 * 1024
+            collective_id=0, has_side_effects=True, vmem_limit_bytes=60 * 1024 * 1024
         ),
     )(
-        features.reshape(OWN, CELLS),
-        cotangent.reshape(OWN, CELLS),
+        features,
+        cotangent,
         filters.reshape(ROWS, C),
     )
-    return (
-        resp.reshape(features.shape),
-        back.reshape(cotangent.shape),
-        grad[:ROWS].reshape(filters.shape),
-    )
+    return resp, back, grad[:ROWS].reshape(filters.shape)
 
 
 def solution(mesh):

time: 52.9 us -> 52.2 us (0.987)
  local copies, waits for them, and re-layouts: 4.19 us -> 3.66 us
    reshape x2 -> x0, local copies, waits for them, and re-layouts: 1.32 us -> none  [the longest x1 0.66 us: shards(): resp.reshape(features.shape)]
    slice x1, local copies, waits for them, and re-layouts: 0.97 us -> 2.17 us  [shards(): return (resp, back, grad[:ROWS].reshape(filters.shape))]
where the time goes in v3:
time: 52.2 us; the launch traced here: 52 us
  Pallas kernels  47.7 us (91%)
  local copies, waits for them, and re-layouts  3.66 us (7%)
  between operations  0.65 us (1%)
    pallas_call x1, Pallas kernels, shards(): pl.pallas_call(kernel, out_shape=(jax.ShapeDtypeStruct((OWN, 2, PLANE), B...  47.7 us
    slice x1, local copies, waits for them, and re-layouts, shards(): return (resp, back, grad[:ROWS].reshape(filters.shape))  2.17 us
    unnamed x6, local copies, waits for them, and re-layouts  1.5 us

profile of v3, /device:TPU:1, one launch (start us, length us, event | category | flops | bytes accessed | tf_op | source)
XLA Modules:
  0.0 52.0 jit_solution(5597322548027057189)
XLA Ops:
  0.6 47.7 %shard_map.58 = (bf16[32,2,512]{2,1,0:T(2,128)(2,1)}, bf16[32,2,512]{2,1,0:T(2,128)(2,1)}, f32[896,256]{1,0:T(8,128)}) custom-call(bf16[32,2,512]{2,1,0:T(2,128)(2,1)} %feat_hbm.1, bf16[32,2,512]{2,1,0:T(2,128)(2,1)} %cot_hbm.1, bf16[864,256]{1,0:T(8,128)(2,1)} %bitcast.3), custom_call_target="tpu_custom_call" | custom-call | tf_op jit(solution)/shard_map/pallas_call | solution.py:397
  48.4 0.0 copy-start.1
  48.4 2.2 %slice.3 = f32[864,256]{1,0:T(8,128)} slice(f32[896,256]{1,0:T(8,128)} %get-tuple-element.8), slice={[0:864], [0:256]} | slice | bytes 1769472 | tf_op jit(solution)/shard_map/slice | solution.py:442
  50.6 0.0 copy-done.1
  50.6 0.0 copy-start
  50.6 0.6 %copy.8 = bf16[32,2,512]{2,1,0:T(2,128)(2,1)} copy(bf16[32,2,512]{2,1,0:T(2,128)(2,1)S(1)} %copy-done.1) | data formatting | bytes 131072
  51.2 0.2 copy-done
  51.4 0.6 %copy.9 = bf16[32,2,512]{2,1,0:T(2,128)(2,1)} copy(bf16[32,2,512]{2,1,0:T(2,128)(2,1)S(1)} %copy-done) | data formatting | bytes 131072
Async XLA Ops:
  48.4 2.2 %copy-start.1 = (bf16[32,2,512]{2,1,0:T(2,128)(2,1)S(1)}, bf16[32,2,512]{2,1,0:T(2,128)(2,1)}, u32[]{:S(2)}) copy-start(bf16[32,2,512]{2,1,0:T(2,128)(2,1)} %get-tuple-element.12) | copy-start | bytes 196612
  50.6 0.9 %copy-start = (bf16[32,2,512]{2,1,0:T(2,128)(2,1)S(1)}, bf16[32,2,512]{2,1,0:T(2,128)(2,1)}, u32[]{:S(2)}) copy-start(bf16[32,2,512]{2,1,0:T(2,128)(2,1)} %get-tuple-element.13) | copy-start | bytes 196612

commit v4 on v3

--- a/solution.py
+++ b/solution.py
@@ -1,3 +1,4 @@
+import functools
 import math
 
 import jax
@@ -34,44 +35,92 @@
     return pl.ds(pl.multiple_of(start, unit), size)
 
 
+def encode(blocks):
+    top = functools.reduce(jnp.maximum, [jnp.abs(block) for block in blocks])
+    scale = jnp.maximum(top * 2.0**-15, 1e-30).astype(BF16)
+    inverse = 1.0 / scale.astype(F32)
+    codes = []
+    for block in blocks:
+        power = block * inverse
+        for _ in range(3):
+            power = power * power
+        codes.append(jnp.where(block < 0, -power, power).astype(BF16))
+    return codes, scale
+
+
+def decode(codes, scale):
+    scale = scale.astype(F32)
+    blocks = []
+    for code in codes:
+        code = code.astype(F32)
+        root = lax.rsqrt(lax.rsqrt(jnp.maximum(jnp.abs(code), 2e-38)))
+        root = root * lax.rsqrt(root) * scale
+        blocks.append(jnp.where(code < 0, -root, root))
+    return blocks
+
+
+def put_rows(ref, value):
+    codes, scale = encode([value[i:i + 16] for i in range(0, CHUNK, 16)])
+    ref[pl.ds(0, CHUNK)] = jnp.concatenate(codes, axis=0)
+    ref[pl.ds(CHUNK, 16)] = scale
+
+
+def get_rows(ref):
+    codes = [ref[pl.ds(i, 16)] for i in range(0, CHUNK, 16)]
+    return jnp.concatenate(decode(codes, ref[pl.ds(CHUNK, 16)]), axis=0)
+
+
+def put_columns(ref, value):
+    codes, scale = encode([value[:, i:i + 128] for i in range(0, CELLS, 128)])
+    ref[:, pl.ds(0, CELLS)] = jnp.concatenate(codes, axis=1)
+    ref[:, pl.ds(CELLS, 128)] = scale
+
+
+def get_columns(ref):
+    codes = [ref[:, pl.ds(i, 128)] for i in range(0, CELLS, 128)]
+    return jnp.concatenate(decode(codes, ref[:, pl.ds(CELLS, 128)]), axis=1)
+
+
 class Ring:
-    def __init__(self, group, chunk, rows, split, pos, nxt, prv, first, both):
-        self.group, self.chunk, self.rows, self.split = group, chunk, rows, split
-        self.pos, self.nxt, self.prv = pos, nxt, prv
-        self.first, self.both = first, both
+    def __init__(self, group, chunks, pos, nxt, prv, out, first, both):
+        self.group, self.chunks, self.pos, self.nxt, self.prv = group, chunks, pos, nxt, prv
+        self.out, self.first, self.both = out, first, both
+
+    def part(self, k, half):
+        return self.chunks[(self.pos + k) % 4, pl.ds(half * 16, 16)]
 
     def start(self):
-        low, high = self.split, self.rows - self.split
-        far, up, down = ((self.pos + k) % 4 for k in (2, 1, 3))
-        self.early = self.group(self.first)
-        self.early.send(self.chunk(far, 0, low), self.first.at[pl.ds(0, low)], self.nxt)
-        self.early.send(self.chunk(far, low, high), self.first.at[pl.ds(low, high)], self.prv)
-        self.late = self.group(self.both)
-        self.late.send(self.chunk(up, low, high), self.both.at[0, pl.ds(low, high)], self.nxt)
-        self.late.send(self.chunk(down, 0, low), self.both.at[1, pl.ds(0, low)], self.prv)
+        self.early, self.late = self.group(self.first), self.group(self.both)
+        put_columns(self.out.at[0], self.part(2, 0))
+        self.early.send(self.out.at[0], self.first.at[0], self.nxt)
+        put_columns(self.out.at[1], self.part(2, 1))
+        self.early.send(self.out.at[1], self.first.at[1], self.prv)
+        put_columns(self.out.at[2], self.part(1, 1))
+        self.late.send(self.out.at[2], self.both.at[0, 1], self.nxt)
+        put_columns(self.out.at[3], self.part(3, 0))
+        self.late.send(self.out.at[3], self.both.at[1, 0], self.prv)
 
     def middle(self):
-        low, high = self.split, self.rows - self.split
-        up, down = ((self.pos + k) % 4 for k in (1, 3))
         self.early.wait_recv()
-        part = self.chunk(up, 0, low)
-        part[...] += self.first[pl.ds(0, low)]
-        self.late.send(part, self.both.at[0, pl.ds(0, low)], self.nxt)
-        part = self.chunk(down, low, high)
-        part[...] += self.first[pl.ds(low, high)]
-        self.late.send(part, self.both.at[1, pl.ds(low, high)], self.prv)
+        put_columns(self.out.at[4], self.part(1, 0) + get_columns(self.first.at[0]))
+        self.late.send(self.out.at[4], self.both.at[0, 0], self.nxt)
+        put_columns(self.out.at[5], self.part(3, 1) + get_columns(self.first.at[1]))
+        self.late.send(self.out.at[5], self.both.at[1, 1], self.prv)
 
     def end(self):
         self.late.wait_recv()
-        return self.chunk(self.pos, 0, self.rows)[...] + self.both[0] + self.both[1]
+        return [
+            self.part(0, half) + get_columns(self.both.at[0, half]) + get_columns(self.both.at[1, half])
+            for half in (0, 1)
+        ]
 
 
 def kernel(
     feat_hbm, cot_hbm, taps_hbm, resp_out, back_out, grad_out,
     feat_raw, cot_raw, taps, taps_t, feat, cot, field, cot_halo, cim,
-    back, back_in, back_sum, back_first, back_both,
+    back, back_in, back_sum, back_code, back_first, back_both,
     z, core_sum, row_sum, resp_in,
-    grad, grad_in, part, part_in, whole,
+    grad, grad_code, grad_in, part, part_in, whole, whole_code, whole_in,
     load_sem, send_sem, recv_sem,
 ):
     loads = [
@@ -229,7 +278,9 @@
             u = half * 2 + r
             sent = Group(grad_in.at[u])
             for k in (2, 1, 3):
-                sent.send(grad.at[half, unit_rows(r, (pos + k) % 4)], grad_in.at[u, k - 1], along(k))
+                code = grad_code.at[u, k - 1]
+                put_rows(code, grad[half, unit_rows(r, (pos + k) % 4)])
+                sent.send(code, grad_in.at[u, k - 1], along(k))
             scattered[u] = sent
 
     def eight(pos, along):
@@ -243,9 +294,10 @@
         for r, (pos, _, pos2, along2) in enumerate(orders):
             u = half * 2 + r
             scattered[u].wait_recv()
-            part[u, pl.ds(0, CHUNK)] = (
-                grad[half, unit_rows(r, pos)] + grad_in[u, 0] + grad_in[u, 1] + grad_in[u, 2]
-            )
+            total = grad[half, unit_rows(r, pos)]
+            for n in range(3):
+                total = total + get_rows(grad_in.at[u, n])
+            part[u, pl.ds(0, CHUNK)] = total
             part[u, pl.ds(CHUNK, 16)] = jnp.zeros((16, 128), F32)
             sent = Group(part_in.at[u])
             for n, device, there in eight(pos2, along2)[1]:
@@ -272,12 +324,23 @@
         for r, (pos, along, _, _) in enumerate(orders):
             u = half * 2 + r
             gathered[u].wait_recv()
-            sent = Group(grad_in.at[u])
-            place = grad_out.at[unit_rows(r, pos), lanes]
+            code = whole_code.at[u]
+            put_rows(code, whole[u, pl.ds(0, CHUNK)])
+            sent = Group(whole_in.at[u])
             for k in (2, 1, 3):
-                sent.send(whole.at[u, pl.ds(0, CHUNK)], place, along(k))
-            place[...] = whole[u, pl.ds(0, CHUNK)]
+                sent.send(code, whole_in.at[u, k - 1], along(k))
+            grad_out[unit_rows(r, pos), lanes] = get_rows(code)
             gathered_again[u] = sent
+
+    def finish(half):
+        lanes = aligned(channels(half), 128, 128)
+        for r, (pos, _, _, _) in enumerate(orders):
+            u = half * 2 + r
+            gathered_again[u].wait_recv()
+
+            @pl.loop(0, 3)
+            def _(n):
+                grad_out[unit_rows(r, (pos + 3 - n) % 4), lanes] = get_rows(whole_in.at[u, n])
 
     scattered, scattered_again, gathered, gathered_again = {}, {}, {}, {}
 
@@ -289,6 +352,14 @@
     filter_products(0)
     scatter(0)
 
+    far_by_other.wait_recv()
+    far_by_pair.wait_recv()
+    far_relay = pass_on(block(owner(far)), sibling)
+    other_relay.wait_recv()
+    far_relay.wait_recv()
+    filter_products(1)
+    scatter(1)
+
     @pl.loop(0, 4)
     def _(n):
         cols = aligned(n * 256, 256, 256)
@@ -296,16 +367,9 @@
             taps_t[...], cim[:, cols], (((1,), (0,)), ((), ())), preferred_element_type=F32
         )
 
-    far_by_other.wait_recv()
-    far_by_pair.wait_recv()
-    far_relay = pass_on(block(owner(far)), sibling)
     to_sibling = Group(back_in)
     for k in range(4):
         to_sibling.send(back.at[aligned((2 * k + 1 - core) * OWN, OWN, OWN)], back_in.at[k], sibling)
-    other_relay.wait_recv()
-    far_relay.wait_recv()
-    filter_products(1)
-    scatter(1)
 
     @pl.loop(0, 4)
     def _(n):
@@ -318,10 +382,7 @@
     for k in range(4):
         back_sum[k] = back[aligned((2 * k + core) * OWN, OWN, OWN)] + back_in[k]
 
-    ring = Ring(
-        Group, lambda i, start, count: back_sum.at[i, pl.ds(start, count)], OWN, 16,
-        zh, along_z(1), along_z(3), back_first, back_both,
-    )
+    ring = Ring(Group, back_sum, zh, along_z(1), along_z(3), back_code, back_first, back_both)
     ring.start()
 
     plane_lane = lane[:, :PLANE]
@@ -383,11 +444,11 @@
     gather(1)
     gather_again(0)
     gather_again(1)
-    total = ring.end().astype(BF16)
-    for d in (0, 1):
-        back_out[:, d, :] = total[:, d * PLANE:(d + 1) * PLANE]
-    for u in range(4):
-        gathered_again[u].wait_recv()
+    for half, total in enumerate(ring.end()):
+        for d in (0, 1):
+            back_out[pl.ds(half * 16, 16), d, :] = total[:, d * PLANE:(d + 1) * PLANE].astype(BF16)
+    finish(0)
+    finish(1)
     for group in groups:
         group.wait_send()
 
@@ -397,9 +458,9 @@
     resp, back, grad = pl.pallas_call(
         kernel,
         out_shape=(
-            jax.ShapeDtypeStruct((OWN, 2, PLANE), BF16),
-            jax.ShapeDtypeStruct((OWN, 2, PLANE), BF16),
-            jax.ShapeDtypeStruct((PADDED, C), F32),
+            pltpu.VMEM((OWN, 2, PLANE), BF16),
+            pltpu.VMEM((OWN, 2, PLANE), BF16),
+            pltpu.VMEM((PADDED, C), F32),
         ),
         in_specs=[pl.BlockSpec(memory_space=pl.ANY)] * 3,
         out_specs=(vmem,) * 3,
@@ -416,17 +477,21 @@
             pltpu.VMEM((C, CELLS), F32),
             pltpu.VMEM((4, OWN, CELLS), F32),
             pltpu.VMEM((4, OWN, CELLS), F32),
-            pltpu.VMEM((OWN, CELLS), F32),
-            pltpu.VMEM((2, OWN, CELLS), F32),
+            pltpu.VMEM((6, 16, CELLS + 128), BF16),
+            pltpu.VMEM((2, 16, CELLS + 128), BF16),
+            pltpu.VMEM((2, 2, 16, CELLS + 128), BF16),
             pltpu.VMEM((ROWS, CELLS), F32),
             pltpu.VMEM((4, OWN, PLANE), F32),
             pltpu.VMEM((4, OWN, 128), F32),
             pltpu.VMEM((OWN, 2 * PLANE + 4 * 128), F32),
             pltpu.VMEM((2, PADDED, 128), F32),
-            pltpu.VMEM((4, 3, CHUNK, 128), F32),
+            pltpu.VMEM((4, 3, CHUNK + 16, 128), BF16),
+            pltpu.VMEM((4, 3, CHUNK + 16, 128), BF16),
             pltpu.VMEM((4, CHUNK + 16, 128), F32),
             pltpu.VMEM((4, 7, 16, 128), F32),
             pltpu.VMEM((4, CHUNK + 16, 128), F32),
+            pltpu.VMEM((4, CHUNK + 16, 128), BF16),
+            pltpu.VMEM((4, 3, CHUNK + 16, 128), BF16),
             pltpu.SemaphoreType.DMA((3,)),
             pltpu.SemaphoreType.DMA((N_GROUPS,)),
             pltpu.SemaphoreType.DMA((N_GROUPS,)),

time: 52.2 us -> 46.9 us (0.90)
  Pallas kernels: 47.7 us -> 43.9 us
  local copies, waits for them, and re-layouts: 3.66 us -> 2.23 us
    pallas_call x1, Pallas kernels: 47.7 us -> 43.9 us  [shards(): pl.pallas_call(kernel, out_shape=(pltpu.VMEM((OWN, 2, PLANE), BF16), pltp...]
    slice x1, local copies, waits for them, and re-layouts: 2.17 us -> 0.97 us  [shards(): return (resp, back, grad[:ROWS].reshape(filters.shape))]
    unnamed x6 -> x2, local copies, waits for them, and re-layouts: 1.5 us -> 1.26 us
where the time goes in v4:
time: 46.9 us; the launch traced here: 46.8 us
  Pallas kernels  43.9 us (94%)
  local copies, waits for them, and re-layouts  2.23 us (5%)
  between operations  0.64 us (1%)
    pallas_call x1, Pallas kernels, shards(): pl.pallas_call(kernel, out_shape=(pltpu.VMEM((OWN, 2, PLANE), BF16), pltp...  43.9 us
    unnamed x2, local copies, waits for them, and re-layouts  1.26 us
    slice x1, local copies, waits for them, and re-layouts, shards(): return (resp, back, grad[:ROWS].reshape(filters.shape))  0.97 us

profile of v4, /device:TPU:1, one launch (start us, length us, event | category | flops | bytes accessed | tf_op | source)
XLA Modules:
  0.0 46.8 jit_solution(8483467717280489929)
XLA Ops:
  0.6 43.9 %shard_map.58 = (bf16[32,2,512]{2,1,0:T(2,128)(2,1)S(1)}, bf16[32,2,512]{2,1,0:T(2,128)(2,1)S(1)}, f32[896,256]{1,0:T(8,128)S(1)}) custom-call(bf16[32,2,512]{2,1,0:T(2,128)(2,1)} %feat_hbm.1, bf16[32,2,512]{2,1,0:T(2,128)(2,1)} %cot_hbm.1, bf16[864,256]{1,0:T(8,128)(2,1)} %bitcast.3), custom_call_target="tpu_custom_call" | custom-call | tf_op jit(solution)/shard_map/pallas_call | solution.py:458
  44.6 0.6 %copy.8 = bf16[32,2,512]{2,1,0:T(2,128)(2,1)} copy(bf16[32,2,512]{2,1,0:T(2,128)(2,1)S(1)} %get-tuple-element.9) | data formatting | bytes 131072
  45.2 0.6 %copy.9 = bf16[32,2,512]{2,1,0:T(2,128)(2,1)} copy(bf16[32,2,512]{2,1,0:T(2,128)(2,1)S(1)} %get-tuple-element.10) | data formatting | bytes 131072
  45.8 1.0 %slice.3 = f32[864,256]{1,0:T(8,128)} slice(f32[896,256]{1,0:T(8,128)S(1)} %get-tuple-element.8), slice={[0:864], [0:256]} | slice | bytes 1769472 | tf_op jit(solution)/shard_map/slice | solution.py:507

commit v5 on v4

--- a/solution.py
+++ b/solution.py
@@ -37,12 +37,12 @@
 
 def encode(blocks):
     top = functools.reduce(jnp.maximum, [jnp.abs(block) for block in blocks])
-    scale = jnp.maximum(top * 2.0**-15, 1e-30).astype(BF16)
+    scale = jnp.maximum(top * 2.0**-7.75, 1e-30).astype(BF16)
     inverse = 1.0 / scale.astype(F32)
     codes = []
     for block in blocks:
         power = block * inverse
-        for _ in range(3):
+        for _ in range(4):
             power = power * power
         codes.append(jnp.where(block < 0, -power, power).astype(BF16))
     return codes, scale
@@ -53,8 +53,10 @@
     blocks = []
     for code in codes:
         code = code.astype(F32)
-        root = lax.rsqrt(lax.rsqrt(jnp.maximum(jnp.abs(code), 2e-38)))
-        root = root * lax.rsqrt(root) * scale
+        root = jnp.maximum(jnp.abs(code), 2e-38)
+        for _ in range(4):
+            root = lax.rsqrt(root)
+        root = jnp.where(code == 0, 0.0, root * scale)
         blocks.append(jnp.where(code < 0, -root, root))
     return blocks
 
@@ -178,12 +180,13 @@
     barrier = pltpu.get_barrier_semaphore()
     for partner in partners:
         pl.semaphore_signal(barrier, inc=1, device_id=partner, device_id_type=MESH)
-    for load, raw, flat in zip(loads, (feat_raw, cot_raw), (feat, cot)):
-        load.wait()
+
+    def lay_flat(n, raw, flat):
+        loads[n].wait()
         for d in (0, 1):
             flat[:, pl.ds(d * PLANE, PLANE)] = raw[:, d, :]
-    loads[2].wait()
-    taps_t[...] = taps[...].T
+
+    lay_flat(0, feat_raw, feat)
     pl.semaphore_wait(barrier, len(partners))
 
     def block(channels_of):
@@ -203,7 +206,9 @@
         return field.at[aligned(owner(k) * OWN + start, 16, 16)]
 
     from_pair = Group(block(af)).send(feat, block(af), along_z(pair))
+    from_other = Group(block(af)).send(feat, block(af), along_z(other))
     from_sibling = Group(block(af)).send(feat, block(af), sibling)
+    lay_flat(1, cot_raw, cot)
 
     edge = (1 - gy) * (PLANE - 128)
     low_edge = cot.at[:, aligned(edge, 128, 128)]
@@ -219,8 +224,9 @@
     halos.send(cot.at[:, pl.ds(PLANE, PLANE)], cot_halo.at[:, pl.ds(0, PLANE)], (d_next, gy, af))
     halos.send(low_edge, halo(1), (gz, side, af))
     halos.send(high_edge, halo(2), (gz, side, af))
-    from_other = Group(block(af)).send(feat, block(af), along_z(other))
     block(af)[...] = feat[...]
+    loads[2].wait()
+    taps_t[...] = taps[...].T
 
     from_pair.wait_recv()
     far_by_other = pass_on(half_block(pair, 0), along_z(other))
@@ -371,19 +377,21 @@
     for k in range(4):
         to_sibling.send(back.at[aligned((2 * k + 1 - core) * OWN, OWN, OWN)], back_in.at[k], sibling)
 
+    scatter_again(0)
+
+    to_sibling.wait_recv()
+    for k in range(4):
+        back_sum[k] = back[aligned((2 * k + core) * OWN, OWN, OWN)] + back_in[k]
+
+    ring = Ring(Group, back_sum, zh, along_z(1), along_z(3), back_code, back_first, back_both)
+    ring.start()
+
     @pl.loop(0, 4)
     def _(n):
         cols = aligned(n * 256, 256, 256)
         z[:, cols] = jnp.dot(taps[...], field[:, cols], preferred_element_type=F32)
 
-    scatter_again(0)
-
-    to_sibling.wait_recv()
-    for k in range(4):
-        back_sum[k] = back[aligned((2 * k + core) * OWN, OWN, OWN)] + back_in[k]
-
-    ring = Ring(Group, back_sum, zh, along_z(1), along_z(3), back_code, back_first, back_both)
-    ring.start()
+    scatter_again(1)
 
     plane_lane = lane[:, :PLANE]
     plane_column = column[:, :PLANE]
@@ -423,10 +431,10 @@
     outer.send(row_sum.at[0], resp_row(3), (d_prev, side, af))
     outer.send(row_sum.at[3], resp_row(2), (d_next, side, af))
 
-    scatter_again(1)
     gather(0)
     ring.middle()
 
+    gather(1)
     outer.wait_recv()
     for d, valid in ((0, gz > 0), (1, gz < 15)):
         total = core_sum[d + 1] + jnp.where(valid, resp_in[:, pl.ds(d * PLANE, PLANE)], 0.0)
@@ -441,16 +449,28 @@
         )
         resp_out[:, d, :] = (total + slab).astype(BF16)
 
-    gather(1)
     gather_again(0)
-    gather_again(1)
     for half, total in enumerate(ring.end()):
         for d in (0, 1):
             back_out[pl.ds(half * 16, 16), d, :] = total[:, d * PLANE:(d + 1) * PLANE].astype(BF16)
+    gather_again(1)
     finish(0)
     finish(1)
     for group in groups:
         group.wait_send()
+
+
+def copy_out(resp, back, grad, resp_out, back_out, grad_out, sem):
+    copies = [
+        pltpu.make_async_copy(src, dst, sem.at[n])
+        for n, (src, dst) in enumerate(
+            ((grad.at[pl.ds(0, ROWS)], grad_out), (resp, resp_out), (back, back_out))
+        )
+    ]
+    for copy in copies:
+        copy.start()
+    for copy in copies:
+        copy.wait()
 
 
 def shards(features, filters, cotangent):
@@ -504,7 +524,18 @@
         cotangent,
         filters.reshape(ROWS, C),
     )
-    return resp, back, grad[:ROWS].reshape(filters.shape)
+    resp, back, grad = pl.pallas_call(
+        copy_out,
+        out_shape=(
+            jax.ShapeDtypeStruct((OWN, 2, PLANE), BF16),
+            jax.ShapeDtypeStruct((OWN, 2, PLANE), BF16),
+            jax.ShapeDtypeStruct((ROWS, C), F32),
+        ),
+        in_specs=[vmem] * 3,
+        out_specs=(pl.BlockSpec(memory_space=pl.ANY),) * 3,
+        scratch_shapes=[pltpu.SemaphoreType.DMA((3,))],
+    )(resp, back, grad)
+    return resp, back, grad.reshape(filters.shape)
 
 
 def solution(mesh):

time: 46.9 us -> 47.6 us (1.015)
  Pallas kernels: 43.9 us -> 44.6 us
    pallas_call x0 -> x1, Pallas kernels: none -> 2.22 us  [shards(): pl.pallas_call(copy_out, out_shape=(jax.ShapeDtypeStruct((OWN, 2, PLANE),...]
    pallas_call x1, Pallas kernels: 43.9 us -> 42.4 us  [shards(): pl.pallas_call(kernel, out_shape=(pltpu.VMEM((OWN, 2, PLANE), BF16), pltp...]
    slice x1 -> x0, local copies, waits for them, and re-layouts: 0.97 us -> none  [shards(): return (resp, back, grad[:ROWS].reshape(filters.shape))]
    unnamed x2 -> x6, local copies, waits for them, and re-layouts: 1.26 us -> 2.18 us
where the time goes in v5:
time: 47.6 us; the launch traced here: 47.4 us
  Pallas kernels  44.6 us (94%)
  local copies, waits for them, and re-layouts  2.18 us (5%)
  between operations  0.65 us (1%)
    pallas_call x1, Pallas kernels, shards(): pl.pallas_call(kernel, out_shape=(pltpu.VMEM((OWN, 2, PLANE), BF16), pltp...  42.4 us
    pallas_call x1, Pallas kernels, shards(): pl.pallas_call(copy_out, out_shape=(jax.ShapeDtypeStruct((OWN, 2, PLANE),...  2.22 us
    unnamed x6, local copies, waits for them, and re-layouts  2.18 us

profile of v5, /device:TPU:1, one launch (start us, length us, event | category | flops | bytes accessed | tf_op | source)
XLA Modules:
  0.0 47.4 jit_solution(6138501561442737919)
XLA Ops:
  0.6 42.4 %shard_map.58 = (bf16[32,2,512]{2,1,0:T(2,128)(2,1)S(1)}, bf16[32,2,512]{2,1,0:T(2,128)(2,1)S(1)}, f32[896,256]{1,0:T(8,128)S(1)}) custom-call(bf16[32,2,512]{2,1,0:T(2,128)(2,1)} %feat_hbm.1, bf16[32,2,512]{2,1,0:T(2,128)(2,1)} %cot_hbm.1, bf16[864,256]{1,0:T(8,128)(2,1)} %bitcast.2), custom_call_target="tpu_custom_call" | custom-call | tf_op jit(solution)/shard_map/pallas_call | solution.py:478
  43.0 0.0 copy-start
  43.0 0.9 %copy-done = f32[896,256]{1,0:T(8,128)} copy-done((f32[896,256]{1,0:T(8,128)}, f32[896,256]{1,0:T(8,128)S(1)}, u32[]{:S(2)}) %copy-start) | copy-done | bytes 917528
  44.0 0.0 copy-start.1
  44.0 0.6 %copy-done.1 = bf16[32,2,512]{2,1,0:T(2,128)(2,1)} copy-done((bf16[32,2,512]{2,1,0:T(2,128)(2,1)}, bf16[32,2,512]{2,1,0:T(2,128)(2,1)S(1)}, u32[]{:S(2)}) %copy-start.1) | copy-done | bytes 65560
  44.6 0.0 copy-start.2
  44.6 0.6 %copy-done.2 = bf16[32,2,512]{2,1,0:T(2,128)(2,1)} copy-done((bf16[32,2,512]{2,1,0:T(2,128)(2,1)}, bf16[32,2,512]{2,1,0:T(2,128)(2,1)S(1)}, u32[]{:S(2)}) %copy-start.2) | copy-done | bytes 65560
  45.2 2.2 %shard_map.59 = (bf16[32,2,512]{2,1,0:T(2,128)(2,1)}, bf16[32,2,512]{2,1,0:T(2,128)(2,1)}, f32[864,256]{1,0:T(8,128)}) custom-call(bf16[32,2,512]{2,1,0:T(2,128)(2,1)} %copy-done.1, bf16[32,2,512]{2,1,0:T(2,128)(2,1)} %copy-done.2, f32[896,256]{1,0:T(8,128)} %copy-done), custom_call_target="tpu_custom_call" | custom-call | tf_op jit(solution)/shard_map/pallas_call | solution.py:527
Async XLA Ops:
  43.0 0.9 %copy-start = (f32[896,256]{1,0:T(8,128)}, f32[896,256]{1,0:T(8,128)S(1)}, u32[]{:S(2)}) copy-start(f32[896,256]{1,0:T(8,128)S(1)} %get-tuple-element.11.grad) | copy-start | bytes 2752516
  44.0 0.6 %copy-start.1 = (bf16[32,2,512]{2,1,0:T(2,128)(2,1)}, bf16[32,2,512]{2,1,0:T(2,128)(2,1)S(1)}, u32[]{:S(2)}) copy-start(bf16[32,2,512]{2,1,0:T(2,128)(2,1)S(1)} %get-tuple-element.9.resp) | copy-start | bytes 196612
  44.6 0.6 %copy-start.2 = (bf16[32,2,512]{2,1,0:T(2,128)(2,1)}, bf16[32,2,512]{2,1,0:T(2,128)(2,1)S(1)}, u32[]{:S(2)}) copy-start(bf16[32,2,512]{2,1,0:T(2,128)(2,1)S(1)} %get-tuple-element.10.back) | copy-start | bytes 196612

commit v6 on v5

--- a/solution.py
+++ b/solution.py
@@ -358,6 +358,24 @@
     filter_products(0)
     scatter(0)
 
+    @pl.loop(0, 4)
+    def _(n):
+        cols = aligned(n * 256, 256, 256)
+        back[:, cols] = lax.dot_general(
+            taps_t[...], cim[:, cols], (((1,), (0,)), ((), ())), preferred_element_type=F32
+        )
+
+    to_sibling = Group(back_in)
+    for k in range(4):
+        to_sibling.send(back.at[aligned((2 * k + 1 - core) * OWN, OWN, OWN)], back_in.at[k], sibling)
+
+    to_sibling.wait_recv()
+    for k in range(4):
+        back_sum[k] = back[aligned((2 * k + core) * OWN, OWN, OWN)] + back_in[k]
+
+    ring = Ring(Group, back_sum, zh, along_z(1), along_z(3), back_code, back_first, back_both)
+    ring.start()
+
     far_by_other.wait_recv()
     far_by_pair.wait_recv()
     far_relay = pass_on(block(owner(far)), sibling)
@@ -366,33 +384,19 @@
     filter_products(1)
     scatter(1)
 
-    @pl.loop(0, 4)
-    def _(n):
-        cols = aligned(n * 256, 256, 256)
-        back[:, cols] = lax.dot_general(
-            taps_t[...], cim[:, cols], (((1,), (0,)), ((), ())), preferred_element_type=F32
-        )
-
-    to_sibling = Group(back_in)
-    for k in range(4):
-        to_sibling.send(back.at[aligned((2 * k + 1 - core) * OWN, OWN, OWN)], back_in.at[k], sibling)
-
     scatter_again(0)
 
-    to_sibling.wait_recv()
-    for k in range(4):
-        back_sum[k] = back[aligned((2 * k + core) * OWN, OWN, OWN)] + back_in[k]
-
-    ring = Ring(Group, back_sum, zh, along_z(1), along_z(3), back_code, back_first, back_both)
-    ring.start()
+    scatter_again(1)
+
+    gather(0)
+    ring.middle()
 
     @pl.loop(0, 4)
     def _(n):
         cols = aligned(n * 256, 256, 256)
         z[:, cols] = jnp.dot(taps[...], field[:, cols], preferred_element_type=F32)
 
-    scatter_again(1)
-
+    gather(1)
     plane_lane = lane[:, :PLANE]
     plane_column = column[:, :PLANE]
     for e in range(4):
@@ -431,10 +435,8 @@
     outer.send(row_sum.at[0], resp_row(3), (d_prev, side, af))
     outer.send(row_sum.at[3], resp_row(2), (d_next, side, af))
 
-    gather(0)
-    ring.middle()
-
-    gather(1)
+    gather_again(0)
+    gather_again(1)
     outer.wait_recv()
     for d, valid in ((0, gz > 0), (1, gz < 15)):
         total = core_sum[d + 1] + jnp.where(valid, resp_in[:, pl.ds(d * PLANE, PLANE)], 0.0)
@@ -449,28 +451,13 @@
         )
         resp_out[:, d, :] = (total + slab).astype(BF16)
 
-    gather_again(0)
     for half, total in enumerate(ring.end()):
         for d in (0, 1):
             back_out[pl.ds(half * 16, 16), d, :] = total[:, d * PLANE:(d + 1) * PLANE].astype(BF16)
-    gather_again(1)
     finish(0)
     finish(1)
     for group in groups:
         group.wait_send()
-
-
-def copy_out(resp, back, grad, resp_out, back_out, grad_out, sem):
-    copies = [
-        pltpu.make_async_copy(src, dst, sem.at[n])
-        for n, (src, dst) in enumerate(
-            ((grad.at[pl.ds(0, ROWS)], grad_out), (resp, resp_out), (back, back_out))
-        )
-    ]
-    for copy in copies:
-        copy.start()
-    for copy in copies:
-        copy.wait()
 
 
 def shards(features, filters, cotangent):
@@ -524,18 +511,7 @@
         cotangent,
         filters.reshape(ROWS, C),
     )
-    resp, back, grad = pl.pallas_call(
-        copy_out,
-        out_shape=(
-            jax.ShapeDtypeStruct((OWN, 2, PLANE), BF16),
-            jax.ShapeDtypeStruct((OWN, 2, PLANE), BF16),
-            jax.ShapeDtypeStruct((ROWS, C), F32),
-        ),
-        in_specs=[vmem] * 3,
-        out_specs=(pl.BlockSpec(memory_space=pl.ANY),) * 3,
-        scratch_shapes=[pltpu.SemaphoreType.DMA((3,))],
-    )(resp, back, grad)
-    return resp, back, grad.reshape(filters.shape)
+    return resp, back, grad[:ROWS].reshape(filters.shape)
 
 
 def solution(mesh):

time: 47.6 us -> 41.9 us (0.88)
  Pallas kernels: 44.6 us -> 38.9 us
    pallas_call x1, Pallas kernels: 42.4 us -> 38.9 us  [shards(): pl.pallas_call(kernel, out_shape=(pltpu.VMEM((OWN, 2, PLANE), BF16), pltp...]
    pallas_call x1 -> x0, Pallas kernels: 2.22 us -> none  [shards(): pl.pallas_call(copy_out, out_shape=(jax.ShapeDtypeStruct((OWN, 2, PLANE),...]
    slice x0 -> x1, local copies, waits for them, and re-layouts: none -> 0.97 us  [shards(): return (resp, back, grad[:ROWS].reshape(filters.shape))]
    unnamed x6 -> x2, local copies, waits for them, and re-layouts: 2.18 us -> 1.26 us
where the time goes in v6:
time: 41.9 us; the launch traced here: 41.8 us
  Pallas kernels  38.9 us (93%)
  local copies, waits for them, and re-layouts  2.23 us (5%)
  between operations  0.64 us (2%)
    pallas_call x1, Pallas kernels, shards(): pl.pallas_call(kernel, out_shape=(pltpu.VMEM((OWN, 2, PLANE), BF16), pltp...  38.9 us
    unnamed x2, local copies, waits for them, and re-layouts  1.26 us
    slice x1, local copies, waits for them, and re-layouts, shards(): return (resp, back, grad[:ROWS].reshape(filters.shape))  0.97 us

profile of v6, /device:TPU:1, one launch (start us, length us, event | category | flops | bytes accessed | tf_op | source)
XLA Modules:
  0.0 41.8 jit_solution(8894987701374247886)
XLA Ops:
  0.6 38.9 %shard_map.58 = (bf16[32,2,512]{2,1,0:T(2,128)(2,1)S(1)}, bf16[32,2,512]{2,1,0:T(2,128)(2,1)S(1)}, f32[896,256]{1,0:T(8,128)S(1)}) custom-call(bf16[32,2,512]{2,1,0:T(2,128)(2,1)} %feat_hbm.1, bf16[32,2,512]{2,1,0:T(2,128)(2,1)} %cot_hbm.1, bf16[864,256]{1,0:T(8,128)(2,1)} %bitcast.3), custom_call_target="tpu_custom_call" | custom-call | tf_op jit(solution)/shard_map/pallas_call | solution.py:465
  39.6 0.6 %copy.8 = bf16[32,2,512]{2,1,0:T(2,128)(2,1)} copy(bf16[32,2,512]{2,1,0:T(2,128)(2,1)S(1)} %get-tuple-element.9) | data formatting | bytes 131072
  40.2 0.6 %copy.9 = bf16[32,2,512]{2,1,0:T(2,128)(2,1)} copy(bf16[32,2,512]{2,1,0:T(2,128)(2,1)S(1)} %get-tuple-element.10) | data formatting | bytes 131072
  40.8 1.0 %slice.3 = f32[864,256]{1,0:T(8,128)} slice(f32[896,256]{1,0:T(8,128)S(1)} %get-tuple-element.8), slice={[0:864], [0:256]} | slice | bytes 1769472 | tf_op jit(solution)/shard_map/slice | solution.py:514

commit v7 on v6

--- a/solution.py
+++ b/solution.py
@@ -20,7 +20,8 @@
 ROWS = TAPS * OWN
 PADDED = 896
 CHUNK = PADDED // 8
-N_GROUPS = 32
+SUB = CHUNK // 8
+N_GROUPS = 31
 
 
 def tap_index(a, b, c):
@@ -72,6 +73,28 @@
     return jnp.concatenate(decode(codes, ref[pl.ds(CHUNK, 16)]), axis=0)
 
 
+def encode_sub(value):
+    valid = lax.broadcasted_iota(jnp.int32, value.shape, 0) < SUB
+    top = jnp.max(jnp.where(valid, jnp.abs(value), 0.0), axis=0, keepdims=True)
+    scale = jnp.maximum(jnp.broadcast_to(top, value.shape) * 2.0**-7.75, 1e-30)
+    scale = scale.astype(BF16).astype(F32)
+    power = value * (1.0 / scale)
+    for _ in range(4):
+        power = power * power
+    return jnp.where(valid, jnp.where(value < 0, -power, power), scale).astype(BF16)
+
+
+def decode_sub(code):
+    scale = jnp.broadcast_to(code.astype(F32)[SUB:SUB + 1], code.shape)
+    return decode([code], scale)[0]
+
+
+def get_subs(ref, rows):
+    for j in range(8):
+        rows[pl.ds(j * SUB, 16)] = decode_sub(ref[j])
+    return rows[pl.ds(0, CHUNK)]
+
+
 def put_columns(ref, value):
     codes, scale = encode([value[:, i:i + 128] for i in range(0, CELLS, 128)])
     ref[:, pl.ds(0, CELLS)] = jnp.concatenate(codes, axis=1)
@@ -122,7 +145,7 @@
     feat_raw, cot_raw, taps, taps_t, feat, cot, field, cot_halo, cim,
     back, back_in, back_sum, back_code, back_first, back_both,
     z, core_sum, row_sum, resp_in,
-    grad, grad_code, grad_in, part, part_in, whole, whole_code, whole_in,
+    grad, grad_code, grad_in, part, part_code, part_in, rows_here, whole_code, whole_in,
     load_sem, send_sem, recv_sem,
 ):
     loads = [
@@ -205,8 +228,12 @@
     def half_block(k, start):
         return field.at[aligned(owner(k) * OWN + start, 16, 16)]
 
-    from_pair = Group(block(af)).send(feat, block(af), along_z(pair))
-    from_other = Group(block(af)).send(feat, block(af), along_z(other))
+    low, high = feat.at[pl.ds(0, 16)], feat.at[pl.ds(16, 16)]
+    low_here, high_here = half_block(0, 0), half_block(0, 16)
+    pair_low = Group(low).send(low, low_here, along_z(pair))
+    other_high = Group(high).send(high, high_here, along_z(other))
+    pair_high = Group(high).send(high, high_here, along_z(pair))
+    other_low = Group(low).send(low, low_here, along_z(other))
     from_sibling = Group(block(af)).send(feat, block(af), sibling)
     lay_flat(1, cot_raw, cot)
 
@@ -228,8 +255,11 @@
     loads[2].wait()
     taps_t[...] = taps[...].T
 
-    from_pair.wait_recv()
+    pair_low.wait_recv()
     far_by_other = pass_on(half_block(pair, 0), along_z(other))
+    other_high.wait_recv()
+    far_by_pair = pass_on(half_block(other, 16), along_z(pair))
+    pair_high.wait_recv()
     pair_relay = pass_on(block(owner(pair)), sibling)
 
     halos.wait_recv()
@@ -303,26 +333,28 @@
             total = grad[half, unit_rows(r, pos)]
             for n in range(3):
                 total = total + get_rows(grad_in.at[u, n])
-            part[u, pl.ds(0, CHUNK)] = total
-            part[u, pl.ds(CHUNK, 16)] = jnp.zeros((16, 128), F32)
+            total = jnp.concatenate([total, jnp.zeros((8, 128), F32)], axis=0)
+            for j in range(8):
+                value = total[j * SUB:j * SUB + 16]
+                part[u, j] = value
+                part_code[u, j] = encode_sub(value)
             sent = Group(part_in.at[u])
             for n, device, there in eight(pos2, along2)[1]:
-                sent.send(part.at[u, aligned(there * 16, 16, 16)], part_in.at[u, n], device)
+                sent.send(part_code.at[u, there], part_in.at[u, n], device)
             scattered_again[u] = sent
 
     def gather(half):
         for r, (_, _, pos2, along2) in enumerate(orders):
             u = half * 2 + r
             mine, others = eight(pos2, along2)
-            rows = aligned(mine * 16, 16, 16)
             scattered_again[u].wait_recv()
-            total = part[u, rows]
+            total = part[u, mine]
             for n in range(7):
-                total = total + part_in[u, n]
-            whole[u, rows] = total * (1.0 / math.sqrt(32768.0))
+                total = total + decode_sub(part_in[u, n])
+            whole_code[u, mine] = encode_sub(total * (1.0 / math.sqrt(32768.0)))
             sent = Group(part_in.at[u])
             for _, device, _ in others:
-                sent.send(whole.at[u, rows], whole.at[u, rows], device)
+                sent.send(whole_code.at[u, mine], whole_code.at[u, mine], device)
             gathered[u] = sent
 
     def gather_again(half):
@@ -330,28 +362,24 @@
         for r, (pos, along, _, _) in enumerate(orders):
             u = half * 2 + r
             gathered[u].wait_recv()
-            code = whole_code.at[u]
-            put_rows(code, whole[u, pl.ds(0, CHUNK)])
             sent = Group(whole_in.at[u])
             for k in (2, 1, 3):
-                sent.send(code, whole_in.at[u, k - 1], along(k))
-            grad_out[unit_rows(r, pos), lanes] = get_rows(code)
+                sent.send(whole_code.at[u], whole_in.at[u, k - 1], along(k))
             gathered_again[u] = sent
+        for r, (pos, along, _, _) in enumerate(orders):
+            grad_out[unit_rows(r, pos), lanes] = get_subs(whole_code.at[half * 2 + r], rows_here)
 
     def finish(half):
         lanes = aligned(channels(half), 128, 128)
         for r, (pos, _, _, _) in enumerate(orders):
             u = half * 2 + r
             gathered_again[u].wait_recv()
-
-            @pl.loop(0, 3)
-            def _(n):
-                grad_out[unit_rows(r, (pos + 3 - n) % 4), lanes] = get_rows(whole_in.at[u, n])
+            for n in range(3):
+                grad_out[unit_rows(r, (pos + 3 - n) % 4), lanes] = get_subs(whole_in.at[u, n], rows_here)
 
     scattered, scattered_again, gathered, gathered_again = {}, {}, {}, {}
 
-    from_other.wait_recv()
-    far_by_pair = pass_on(half_block(other, 16), along_z(pair))
+    other_low.wait_recv()
     other_relay = pass_on(block(owner(other)), sibling)
     from_sibling.wait_recv()
     pair_relay.wait_recv()
@@ -494,11 +522,12 @@
             pltpu.VMEM((2, PADDED, 128), F32),
             pltpu.VMEM((4, 3, CHUNK + 16, 128), BF16),
             pltpu.VMEM((4, 3, CHUNK + 16, 128), BF16),
-            pltpu.VMEM((4, CHUNK + 16, 128), F32),
-            pltpu.VMEM((4, 7, 16, 128), F32),
-            pltpu.VMEM((4, CHUNK + 16, 128), F32),
-            pltpu.VMEM((4, CHUNK + 16, 128), BF16),
-            pltpu.VMEM((4, 3, CHUNK + 16, 128), BF16),
+            pltpu.VMEM((4, 8, 16, 128), F32),
+            pltpu.VMEM((4, 8, 16, 128), BF16),
+            pltpu.VMEM((4, 7, 16, 128), BF16),
+            pltpu.VMEM((CHUNK + 16, 128), F32),
+            pltpu.VMEM((4, 8, 16, 128), BF16),
+            pltpu.VMEM((4, 3, 8, 16, 128), BF16),
             pltpu.SemaphoreType.DMA((3,)),
             pltpu.SemaphoreType.DMA((N_GROUPS,)),
             pltpu.SemaphoreType.DMA((N_GROUPS,)),

time: 41.9 us -> 41 us (0.979); the launches traced: 41.8 us -> 40.5 us
  Pallas kernels: 38.9 us -> 37.6 us
    pallas_call x1, Pallas kernels: 38.9 us -> 37.6 us  [shards(): pl.pallas_call(kernel, out_shape=(pltpu.VMEM((OWN, 2, PLANE), BF16), pltp...]
where the time goes in v7:
time: 41 us; the launch traced here: 40.5 us
  Pallas kernels  37.6 us (92%)
  local copies, waits for them, and re-layouts  2.23 us (5%)
  between operations  0.64 us (2%)
    pallas_call x1, Pallas kernels, shards(): pl.pallas_call(kernel, out_shape=(pltpu.VMEM((OWN, 2, PLANE), BF16), pltp...  37.6 us
    unnamed x2, local copies, waits for them, and re-layouts  1.26 us
    slice x1, local copies, waits for them, and re-layouts, shards(): return (resp, back, grad[:ROWS].reshape(filters.shape))  0.97 us

profile of v7, /device:TPU:1, one launch (start us, length us, event | category | flops | bytes accessed | tf_op | source)
XLA Modules:
  0.0 40.5 jit_solution(5380408648656136885)
XLA Ops:
  0.6 37.6 %shard_map.58 = (bf16[32,2,512]{2,1,0:T(2,128)(2,1)S(1)}, bf16[32,2,512]{2,1,0:T(2,128)(2,1)S(1)}, f32[896,256]{1,0:T(8,128)S(1)}) custom-call(bf16[32,2,512]{2,1,0:T(2,128)(2,1)} %feat_hbm.1, bf16[32,2,512]{2,1,0:T(2,128)(2,1)} %cot_hbm.1, bf16[864,256]{1,0:T(8,128)(2,1)} %bitcast.3), custom_call_target="tpu_custom_call" | custom-call | tf_op jit(solution)/shard_map/pallas_call | solution.py:493
  38.2 0.6 %copy.8 = bf16[32,2,512]{2,1,0:T(2,128)(2,1)} copy(bf16[32,2,512]{2,1,0:T(2,128)(2,1)S(1)} %get-tuple-element.9) | data formatting | bytes 131072
  38.9 0.6 %copy.9 = bf16[32,2,512]{2,1,0:T(2,128)(2,1)} copy(bf16[32,2,512]{2,1,0:T(2,128)(2,1)S(1)} %get-tuple-element.10) | data formatting | bytes 131072
  39.5 1.0 %slice.3 = f32[864,256]{1,0:T(8,128)} slice(f32[896,256]{1,0:T(8,128)S(1)} %get-tuple-element.8), slice={[0:864], [0:256]} | slice | bytes 1769472 | tf_op jit(solution)/shard_map/slice | solution.py:543

commit v8 on v7

--- a/solution.py
+++ b/solution.py
@@ -21,7 +21,7 @@
 PADDED = 896
 CHUNK = PADDED // 8
 SUB = CHUNK // 8
-N_GROUPS = 31
+N_GROUPS = 35
 
 
 def tap_index(a, b, c):
@@ -164,14 +164,14 @@
     d_next, d_prev = (gz + 1) % 16, (gz + 15) % 16
     side = 1 - gy
 
-    def along_x(k, row=gy):
-        return (py * 4 + (px + k) % 4, row, af)
-
-    def along_y(k, row=gy):
-        return (((py + k) % 4) * 4 + px, row, af)
-
-    def along_z(k):
-        return (gz, gy, ((zh + k) % 4) * 2 + core)
+    def along_x(k, row=gy, to=core):
+        return (py * 4 + (px + k) % 4, row, zh * 2 + to)
+
+    def along_y(k, row=gy, to=core):
+        return (((py + k) % 4) * 4 + px, row, zh * 2 + to)
+
+    def along_z(k, to=core):
+        return (gz, gy, ((zh + k) % 4) * 2 + to)
 
     groups = []
 
@@ -180,26 +180,29 @@
             self.index, self.size = len(groups), size
             groups.append(self)
 
-        def send(self, src, dst, device):
+        def send(self, src, dst, device, there=None):
+            there = self.index if there is None else there
             pltpu.make_async_remote_copy(
                 src_ref=src, dst_ref=dst,
-                send_sem=send_sem.at[self.index], recv_sem=recv_sem.at[self.index],
+                send_sem=send_sem.at[self.index], recv_sem=recv_sem.at[there],
                 device_id=device, device_id_type=MESH,
             ).start()
             return self
 
-        def wait_recv(self):
-            pltpu.make_async_copy(self.size, self.size, recv_sem.at[self.index]).wait()
+        def wait_recv(self, size=None):
+            size = self.size if size is None else size
+            pltpu.make_async_copy(size, size, recv_sem.at[self.index]).wait()
 
         def wait_send(self):
             pltpu.make_async_copy(self.size, self.size, send_sem.at[self.index]).wait()
 
     partners = [sibling, (d_next, gy, af), (d_prev, gy, af)]
     partners += [(d_next, side, af), (d_prev, side, af), (gz, side, af)]
-    partners += [along_z(1), along_z(3)]
+    for k in (1, 3):
+        partners += [along_z(k), along_z(k, 1 - core)]
     for k in (1, 2, 3):
         for along in (along_x, along_y):
-            partners += [along(k), along(k, side)]
+            partners += [along(k), along(k, side), along(k, gy, 1 - core)]
     barrier = pltpu.get_barrier_semaphore()
     for partner in partners:
         pl.semaphore_signal(barrier, inc=1, device_id=partner, device_id_type=MESH)
@@ -219,21 +222,16 @@
     other = 4 - pair
     far = 2
 
-    def owner(k):
-        return ((zh + k) % 4) * 2 + core
-
-    def pass_on(rows, device):
-        return Group(rows).send(rows, rows, device)
-
-    def half_block(k, start):
-        return field.at[aligned(owner(k) * OWN + start, 16, 16)]
-
-    low, high = feat.at[pl.ds(0, 16)], feat.at[pl.ds(16, 16)]
-    low_here, high_here = half_block(0, 0), half_block(0, 16)
-    pair_low = Group(low).send(low, low_here, along_z(pair))
-    other_high = Group(high).send(high, high_here, along_z(other))
-    pair_high = Group(high).send(high, high_here, along_z(pair))
-    other_low = Group(low).send(low, low_here, along_z(other))
+    def of_chip(k, number):
+        return block(((zh + k) % 4) * 2 + number)
+
+    early = [Group(feat), Group(feat)]
+    late = [Group(feat), Group(feat)]
+    from_far = [Group(feat), Group(feat)]
+    relays = [Group(field.at[pl.ds(0, 2 * OWN)]) for _ in range(3)]
+    k_early = pair + core * (other - pair)
+    early[0].send(feat, block(af), along_z(k_early, 1), early[0].index + core)
+    late[0].send(feat, block(af), along_z(4 - k_early, 1), late[0].index + core)
     from_sibling = Group(block(af)).send(feat, block(af), sibling)
     lay_flat(1, cot_raw, cot)
 
@@ -255,12 +253,19 @@
     loads[2].wait()
     taps_t[...] = taps[...].T
 
-    pair_low.wait_recv()
-    far_by_other = pass_on(half_block(pair, 0), along_z(other))
-    other_high.wait_recv()
-    far_by_pair = pass_on(half_block(other, 16), along_z(pair))
-    pair_high.wait_recv()
-    pair_relay = pass_on(block(owner(pair)), sibling)
+    def relay(n, k, number):
+        rows = of_chip(k, number)
+        relays[n].send(rows, rows, sibling)
+
+    @pl.when(core == 1)
+    def _():
+        for n, k, back in ((0, pair, other), (1, other, pair)):
+            early[n].wait_recv()
+            rows = of_chip(k, n)
+            from_far[n].send(rows, rows, along_z(back))
+            relay(n, k, n)
+        late[1].wait_recv()
+        relay(0, pair, 1)
 
     halos.wait_recv()
     lane = lax.broadcasted_iota(jnp.int32, (OWN, PLANE + 128), 1)
@@ -292,10 +297,8 @@
                     piece = {-1: tall[:, 128:], 0: moved[:, :PLANE], 1: tall[:, :PLANE]}[b]
                     cim[pl.ds(tap_index(a, b, c) * OWN, OWN), pl.ds(d * PLANE, PLANE)] = piece
 
-    near_lanes = (zh // 2) * 128
-
     def channels(half):
-        return near_lanes if half == 0 else 128 - near_lanes
+        return ((zh // 2 + half) % 2) * 128
 
     def filter_products(half):
         grad[half, pl.ds(0, ROWS)] = lax.dot_general(
@@ -309,15 +312,25 @@
     def unit_rows(r, i):
         return aligned(r * 4 * CHUNK + i * CHUNK, CHUNK, 16)
 
+    units = [(mine, r) for mine in (0, 1) for r in (0, 1)]
+    first = [Group(grad_in.at[0, r, pl.ds(1, 3)]) for half, r in units]
+    from_here = [Group(grad_code.at[0, 0]) for half, r in units]
+
     def scatter(half):
+        relation = (core + half) % 2
         for r, (pos, along, _, _) in enumerate(orders):
-            u = half * 2 + r
-            sent = Group(grad_in.at[u])
+            n = half * 2 + r
+            there = first[0].index + relation * 2 + r
             for k in (2, 1, 3):
-                code = grad_code.at[u, k - 1]
+                code = grad_code.at[n, k]
                 put_rows(code, grad[half, unit_rows(r, (pos + k) % 4)])
-                sent.send(code, grad_in.at[u, k - 1], along(k))
-            scattered[u] = sent
+                first[n].send(code, grad_in.at[relation, r, k], along(k, gy, half), there)
+
+            @pl.when(core != half)
+            def _():
+                code = grad_code.at[n, 0]
+                put_rows(code, grad[half, unit_rows(r, pos)])
+                from_here[n].send(code, grad_in.at[1, r, 0], sibling, there)
 
     def eight(pos, along):
         others = []
@@ -326,13 +339,16 @@
             others.append((step - 1, along(k, row), ((pos + k) % 4) * 2 + row))
         return pos * 2 + gy, others
 
-    def scatter_again(half):
-        for r, (pos, _, pos2, along2) in enumerate(orders):
-            u = half * 2 + r
-            scattered[u].wait_recv()
-            total = grad[half, unit_rows(r, pos)]
-            for n in range(3):
-                total = total + get_rows(grad_in.at[u, n])
+    def received(ref, mine, r):
+        return ref.at[1, r] if mine else ref.at[0, r, pl.ds(1, 3)]
+
+    def scatter_again():
+        for u, (mine, r) in enumerate(units):
+            pos, _, pos2, along2 = orders[r]
+            first[u].wait_recv(received(grad_in, mine, r))
+            total = get_rows(grad_in.at[mine, r, 0]) if mine else grad[core, unit_rows(r, pos)]
+            for k in (1, 2, 3):
+                total = total + get_rows(grad_in.at[mine, r, k])
             total = jnp.concatenate([total, jnp.zeros((8, 128), F32)], axis=0)
             for j in range(8):
                 value = total[j * SUB:j * SUB + 16]
@@ -343,46 +359,52 @@
                 sent.send(part_code.at[u, there], part_in.at[u, n], device)
             scattered_again[u] = sent
 
-    def gather(half):
-        for r, (_, _, pos2, along2) in enumerate(orders):
-            u = half * 2 + r
-            mine, others = eight(pos2, along2)
+    def gather():
+        for u, (mine, r) in enumerate(units):
+            _, _, pos2, along2 = orders[r]
+            place, others = eight(pos2, along2)
             scattered_again[u].wait_recv()
-            total = part[u, mine]
+            total = part[u, place]
             for n in range(7):
                 total = total + decode_sub(part_in[u, n])
-            whole_code[u, mine] = encode_sub(total * (1.0 / math.sqrt(32768.0)))
+            whole_code[u, place] = encode_sub(total * (1.0 / math.sqrt(32768.0)))
             sent = Group(part_in.at[u])
             for _, device, _ in others:
-                sent.send(whole_code.at[u, mine], whole_code.at[u, mine], device)
+                sent.send(whole_code.at[u, place], whole_code.at[u, place], device)
             gathered[u] = sent
 
-    def gather_again(half):
-        lanes = aligned(channels(half), 128, 128)
-        for r, (pos, along, _, _) in enumerate(orders):
-            u = half * 2 + r
+    def gather_again():
+        for u, (mine, r) in enumerate(units):
+            along = orders[r][1]
             gathered[u].wait_recv()
-            sent = Group(whole_in.at[u])
+            sent = Group(received(whole_in, mine, r))
             for k in (2, 1, 3):
-                sent.send(whole_code.at[u], whole_in.at[u, k - 1], along(k))
+                sent.send(whole_code.at[u], whole_in.at[mine, r, k], along(k, gy, (core + mine) % 2))
+            if mine:
+                sent.send(whole_code.at[u], whole_in.at[1, r, 0], sibling)
             gathered_again[u] = sent
-        for r, (pos, along, _, _) in enumerate(orders):
-            grad_out[unit_rows(r, pos), lanes] = get_subs(whole_code.at[half * 2 + r], rows_here)
-
-    def finish(half):
-        lanes = aligned(channels(half), 128, 128)
-        for r, (pos, _, _, _) in enumerate(orders):
-            u = half * 2 + r
+
+    def store(mine, r, k, ref):
+        lanes = aligned(channels((core + mine) % 2), 128, 128)
+        grad_out[unit_rows(r, (orders[r][0] + 4 - k) % 4), lanes] = get_subs(ref, rows_here)
+
+    def finish():
+        for r in (0, 1):
+            store(0, r, 0, whole_code.at[r])
+        for u, (mine, r) in enumerate(units):
             gathered_again[u].wait_recv()
-            for n in range(3):
-                grad_out[unit_rows(r, (pos + 3 - n) % 4), lanes] = get_subs(whole_in.at[u, n], rows_here)
-
-    scattered, scattered_again, gathered, gathered_again = {}, {}, {}, {}
-
-    other_low.wait_recv()
-    other_relay = pass_on(block(owner(other)), sibling)
+            for k in range(1 - mine, 4):
+                store(mine, r, k, whole_in.at[mine, r, k])
+
+    scattered_again, gathered, gathered_again = {}, {}, {}
+
+    @pl.when(core == 1)
+    def _():
+        late[0].wait_recv()
+        relay(1, other, 0)
+
+    pl.when(core == 0)(relays[0].wait_recv)
     from_sibling.wait_recv()
-    pair_relay.wait_recv()
     filter_products(0)
     scatter(0)
 
@@ -397,6 +419,20 @@
     for k in range(4):
         to_sibling.send(back.at[aligned((2 * k + 1 - core) * OWN, OWN, OWN)], back_in.at[k], sibling)
 
+    @pl.when(core == 1)
+    def _():
+        for n in (0, 1):
+            from_far[n].wait_recv()
+            relay(2, far, n)
+
+    @pl.when(core == 0)
+    def _():
+        relays[1].wait_recv()
+        relays[2].wait_recv()
+
+    filter_products(1)
+    scatter(1)
+
     to_sibling.wait_recv()
     for k in range(4):
         back_sum[k] = back[aligned((2 * k + core) * OWN, OWN, OWN)] + back_in[k]
@@ -404,27 +440,13 @@
     ring = Ring(Group, back_sum, zh, along_z(1), along_z(3), back_code, back_first, back_both)
     ring.start()
 
-    far_by_other.wait_recv()
-    far_by_pair.wait_recv()
-    far_relay = pass_on(block(owner(far)), sibling)
-    other_relay.wait_recv()
-    far_relay.wait_recv()
-    filter_products(1)
-    scatter(1)
-
-    scatter_again(0)
-
-    scatter_again(1)
-
-    gather(0)
-    ring.middle()
+    scatter_again()
 
     @pl.loop(0, 4)
     def _(n):
         cols = aligned(n * 256, 256, 256)
         z[:, cols] = jnp.dot(taps[...], field[:, cols], preferred_element_type=F32)
 
-    gather(1)
     plane_lane = lane[:, :PLANE]
     plane_column = column[:, :PLANE]
     for e in range(4):
@@ -463,8 +485,12 @@
     outer.send(row_sum.at[0], resp_row(3), (d_prev, side, af))
     outer.send(row_sum.at[3], resp_row(2), (d_next, side, af))
 
-    gather_again(0)
-    gather_again(1)
+    gather()
+
+    ring.middle()
+
+    gather_again()
+
     outer.wait_recv()
     for d, valid in ((0, gz > 0), (1, gz < 15)):
         total = core_sum[d + 1] + jnp.where(valid, resp_in[:, pl.ds(d * PLANE, PLANE)], 0.0)
@@ -482,10 +508,19 @@
     for half, total in enumerate(ring.end()):
         for d in (0, 1):
             back_out[pl.ds(half * 16, 16), d, :] = total[:, d * PLANE:(d + 1) * PLANE].astype(BF16)
-    finish(0)
-    finish(1)
+
+    finish()
+
+    for n, (half, r) in enumerate(units):
+        pl.when(core != half)(from_here[n].wait_send)
+    @pl.when(core == 1)
+    def _():
+        for group in from_far + relays:
+            group.wait_send()
+
     for group in groups:
-        group.wait_send()
+        if group not in from_here + from_far + relays + [early[1], late[1]]:
+            group.wait_send()
 
 
 def shards(features, filters, cotangent):
@@ -520,14 +555,14 @@
             pltpu.VMEM((4, OWN, 128), F32),
             pltpu.VMEM((OWN, 2 * PLANE + 4 * 128), F32),
             pltpu.VMEM((2, PADDED, 128), F32),
-            pltpu.VMEM((4, 3, CHUNK + 16, 128), BF16),
-            pltpu.VMEM((4, 3, CHUNK + 16, 128), BF16),
+            pltpu.VMEM((4, 4, CHUNK + 16, 128), BF16),
+            pltpu.VMEM((2, 2, 4, CHUNK + 16, 128), BF16),
             pltpu.VMEM((4, 8, 16, 128), F32),
             pltpu.VMEM((4, 8, 16, 128), BF16),
             pltpu.VMEM((4, 7, 16, 128), BF16),
             pltpu.VMEM((CHUNK + 16, 128), F32),
             pltpu.VMEM((4, 8, 16, 128), BF16),
-            pltpu.VMEM((4, 3, 8, 16, 128), BF16),
+            pltpu.VMEM((2, 2, 4, 8, 16, 128), BF16),
             pltpu.SemaphoreType.DMA((3,)),
             pltpu.SemaphoreType.DMA((N_GROUPS,)),
             pltpu.SemaphoreType.DMA((N_GROUPS,)),

time: 41 us -> 41 us (level)
  no operation moved by 1% of the time
where the time goes in v8:
time: 41 us; the launch traced here: 40.9 us
  Pallas kernels  38 us (93%)
  local copies, waits for them, and re-layouts  2.23 us (5%)
  between operations  0.64 us (2%)
    pallas_call x1, Pallas kernels, shards(): pl.pallas_call(kernel, out_shape=(pltpu.VMEM((OWN, 2, PLANE), BF16), pltp...  38 us
    unnamed x2, local copies, waits for them, and re-layouts  1.26 us
    slice x1, local copies, waits for them, and re-layouts, shards(): return (resp, back, grad[:ROWS].reshape(filters.shape))  0.97 us

profile of v8, /device:TPU:1, one launch (start us, length us, event | category | flops | bytes accessed | tf_op | source)
XLA Modules:
  0.0 40.9 jit_solution(1938648030028195656)
XLA Ops:
  0.6 38.0 %shard_map.58 = (bf16[32,2,512]{2,1,0:T(2,128)(2,1)S(1)}, bf16[32,2,512]{2,1,0:T(2,128)(2,1)S(1)}, f32[896,256]{1,0:T(8,128)S(1)}) custom-call(bf16[32,2,512]{2,1,0:T(2,128)(2,1)} %feat_hbm.1, bf16[32,2,512]{2,1,0:T(2,128)(2,1)} %cot_hbm.1, bf16[864,256]{1,0:T(8,128)(2,1)} %bitcast.3), custom_call_target="tpu_custom_call" | custom-call | tf_op jit(solution)/shard_map/pallas_call | solution.py:528
  38.6 0.6 %copy.8 = bf16[32,2,512]{2,1,0:T(2,128)(2,1)} copy(bf16[32,2,512]{2,1,0:T(2,128)(2,1)S(1)} %get-tuple-element.9) | data formatting | bytes 131072
  39.3 0.6 %copy.9 = bf16[32,2,512]{2,1,0:T(2,128)(2,1)} copy(bf16[32,2,512]{2,1,0:T(2,128)(2,1)S(1)} %get-tuple-element.10) | data formatting | bytes 131072
  39.9 1.0 %slice.3 = f32[864,256]{1,0:T(8,128)} slice(f32[896,256]{1,0:T(8,128)S(1)} %get-tuple-element.8), slice={[0:864], [0:256]} | slice | bytes 1769472 | tf_op jit(solution)/shard_map/slice | solution.py:578

commit v9 on v8

--- a/solution.py
+++ b/solution.py
@@ -141,7 +141,7 @@
 
 
 def kernel(
-    feat_hbm, cot_hbm, taps_hbm, resp_out, back_out, grad_out,
+    feat_hbm, cot_hbm, taps_hbm, both_out, grad_out,
     feat_raw, cot_raw, taps, taps_t, feat, cot, field, cot_halo, cim,
     back, back_in, back_sum, back_code, back_first, back_both,
     z, core_sum, row_sum, resp_in,
@@ -503,11 +503,11 @@
             ],
             axis=1,
         )
-        resp_out[:, d, :] = (total + slab).astype(BF16)
+        both_out[0, :, d, :] = (total + slab).astype(BF16)
 
     for half, total in enumerate(ring.end()):
         for d in (0, 1):
-            back_out[pl.ds(half * 16, 16), d, :] = total[:, d * PLANE:(d + 1) * PLANE].astype(BF16)
+            both_out[1, pl.ds(half * 16, 16), d, :] = total[:, d * PLANE:(d + 1) * PLANE].astype(BF16)
 
     finish()
 
@@ -525,15 +525,14 @@
 
 def shards(features, filters, cotangent):
     vmem = pl.BlockSpec(memory_space=pltpu.VMEM)
-    resp, back, grad = pl.pallas_call(
+    both, grad = pl.pallas_call(
         kernel,
         out_shape=(
-            pltpu.VMEM((OWN, 2, PLANE), BF16),
-            pltpu.VMEM((OWN, 2, PLANE), BF16),
+            pltpu.VMEM((2, OWN, 2, PLANE), BF16),
             pltpu.VMEM((PADDED, C), F32),
         ),
         in_specs=[pl.BlockSpec(memory_space=pl.ANY)] * 3,
-        out_specs=(vmem,) * 3,
+        out_specs=(vmem,) * 2,
         scratch_shapes=[
             pltpu.VMEM((OWN, 2, PLANE), BF16),
             pltpu.VMEM((OWN, 2, PLANE), BF16),
@@ -575,7 +574,7 @@
         cotangent,
         filters.reshape(ROWS, C),
     )
-    return resp, back, grad[:ROWS].reshape(filters.shape)
+    return both[0], both[1], grad[:ROWS].reshape(filters.shape)
 
 
 def solution(mesh):

time: 41 us -> 40.4 us (0.985)
  local copies, waits for them, and re-layouts: 2.23 us -> 1.71 us
    unnamed x2 -> x0, local copies, waits for them, and re-layouts: 1.26 us -> none
    squeeze x0 -> x1, local copies, waits for them, and re-layouts: none -> 0.74 us  [shards(): return (both[0], both[1], grad[:ROWS].reshape(filters.shape))]
where the time goes in v9:
time: 40.4 us; the launch traced here: 40.3 us
  Pallas kernels  38 us (94%)
  local copies, waits for them, and re-layouts  1.71 us (4%)
  between operations  0.64 us (2%)
    pallas_call x1, Pallas kernels, shards(): pl.pallas_call(kernel, out_shape=(pltpu.VMEM((2, OWN, 2, PLANE), BF16), p...  38 us
    slice x1, local copies, waits for them, and re-layouts, shards(): return (both[0], both[1], grad[:ROWS].reshape(filters.shape))  0.97 us

profile of v9, /device:TPU:1, one launch (start us, length us, event | category | flops | bytes accessed | tf_op | source)
XLA Modules:
  0.0 40.3 jit_solution(9830036151999829170)
XLA Ops:
  0.6 38.0 %shard_map.58 = (bf16[2,32,2,512]{3,2,1,0:T(2,128)(2,1)S(1)}, f32[896,256]{1,0:T(8,128)S(1)}) custom-call(bf16[32,2,512]{2,1,0:T(2,128)(2,1)} %feat_hbm.1, bf16[32,2,512]{2,1,0:T(2,128)(2,1)} %cot_hbm.1, bf16[864,256]{1,0:T(8,128)(2,1)} %bitcast.7), custom_call_target="tpu_custom_call" | custom-call | tf_op jit(solution)/shard_map/pallas_call | solution.py:528
  38.6 0.7 %slice_bitcast_fusion = (bf16[32,2,512]{2,1,0:T(2,128)(2,1)}, bf16[32,2,512]{2,1,0:T(2,128)(2,1)}) fusion(bf16[2,32,2,512]{3,2,1,0:T(2,128)(2,1)S(1)} %get-tuple-element.5), kind=kLoop, calls=%fused_computation | loop fusion | bytes 262144 | tf_op jit(solution)/shard_map/squeeze | solution.py:577
  39.4 1.0 %slice.11 = f32[864,256]{1,0:T(8,128)} slice(f32[896,256]{1,0:T(8,128)S(1)} %get-tuple-element.6), slice={[0:864], [0:256]} | slice | bytes 1769472 | tf_op jit(solution)/shard_map/slice | solution.py:577

commit v10 on v9

--- a/solution.py
+++ b/solution.py
@@ -54,9 +54,7 @@
     blocks = []
     for code in codes:
         code = code.astype(F32)
-        root = jnp.maximum(jnp.abs(code), 2e-38)
-        for _ in range(4):
-            root = lax.rsqrt(root)
+        root = jnp.exp2(jnp.log2(jnp.maximum(jnp.abs(code), 2e-38)) * (1 / 16))
         root = jnp.where(code == 0, 0.0, root * scale)
         blocks.append(jnp.where(code < 0, -root, root))
     return blocks
@@ -110,12 +108,12 @@
     def __init__(self, group, chunks, pos, nxt, prv, out, first, both):
         self.group, self.chunks, self.pos, self.nxt, self.prv = group, chunks, pos, nxt, prv
         self.out, self.first, self.both = out, first, both
+        self.early, self.late = group(first), group(both)
 
     def part(self, k, half):
         return self.chunks[(self.pos + k) % 4, pl.ds(half * 16, 16)]
 
     def start(self):
-        self.early, self.late = self.group(self.first), self.group(self.both)
         put_columns(self.out.at[0], self.part(2, 0))
         self.early.send(self.out.at[0], self.first.at[0], self.nxt)
         put_columns(self.out.at[1], self.part(2, 1))
@@ -433,14 +431,17 @@
     filter_products(1)
     scatter(1)
 
-    to_sibling.wait_recv()
-    for k in range(4):
-        back_sum[k] = back[aligned((2 * k + core) * OWN, OWN, OWN)] + back_in[k]
-
     ring = Ring(Group, back_sum, zh, along_z(1), along_z(3), back_code, back_first, back_both)
-    ring.start()
-
+
+    def start_ring():
+        to_sibling.wait_recv()
+        for k in range(4):
+            back_sum[k] = back[aligned((2 * k + core) * OWN, OWN, OWN)] + back_in[k]
+        ring.start()
+
+    pl.when(core == 1)(start_ring)
     scatter_again()
+    pl.when(core == 0)(start_ring)
 
     @pl.loop(0, 4)
     def _(n):

time: 40.4 us -> 40.2 us (level)
  no operation moved by 1% of the time
where the time goes in v10:
time: 40.2 us; the launch traced here: 40.1 us
  Pallas kernels  37.8 us (94%)
  local copies, waits for them, and re-layouts  1.71 us (4%)
  between operations  0.64 us (2%)
    pallas_call x1, Pallas kernels, shards(): pl.pallas_call(kernel, out_shape=(pltpu.VMEM((2, OWN, 2, PLANE), BF16), p...  37.8 us
    slice x1, local copies, waits for them, and re-layouts, shards(): return (both[0], both[1], grad[:ROWS].reshape(filters.shape))  0.97 us

profile of v10, /device:TPU:1, one launch (start us, length us, event | category | flops | bytes accessed | tf_op | source)
XLA Modules:
  0.0 40.1 jit_solution(6185667597548898201)
XLA Ops:
  0.6 37.8 %shard_map.58 = (bf16[2,32,2,512]{3,2,1,0:T(2,128)(2,1)S(1)}, f32[896,256]{1,0:T(8,128)S(1)}) custom-call(bf16[32,2,512]{2,1,0:T(2,128)(2,1)} %feat_hbm.1, bf16[32,2,512]{2,1,0:T(2,128)(2,1)} %cot_hbm.1, bf16[864,256]{1,0:T(8,128)(2,1)} %bitcast.7), custom_call_target="tpu_custom_call" | custom-call | tf_op jit(solution)/shard_map/pallas_call | solution.py:529
  38.4 0.7 %slice_bitcast_fusion = (bf16[32,2,512]{2,1,0:T(2,128)(2,1)}, bf16[32,2,512]{2,1,0:T(2,128)(2,1)}) fusion(bf16[2,32,2,512]{3,2,1,0:T(2,128)(2,1)S(1)} %get-tuple-element.5), kind=kLoop, calls=%fused_computation | loop fusion | bytes 262144 | tf_op jit(solution)/shard_map/squeeze | solution.py:578
  39.2 1.0 %slice.11 = f32[864,256]{1,0:T(8,128)} slice(f32[896,256]{1,0:T(8,128)S(1)} %get-tuple-element.6), slice={[0:864], [0:256]} | slice | bytes 1769472 | tf_op jit(solution)/shard_map/slice | solution.py:578

commit v11 on v10

--- a/solution.py
+++ b/solution.py
@@ -380,19 +380,20 @@
                 sent.send(whole_code.at[u], whole_in.at[mine, r, k], along(k, gy, (core + mine) % 2))
             if mine:
                 sent.send(whole_code.at[u], whole_in.at[1, r, 0], sibling)
+            else:
+                whole_in[0, r, 0] = whole_code[u]
             gathered_again[u] = sent
 
-    def store(mine, r, k, ref):
-        lanes = aligned(channels((core + mine) % 2), 128, 128)
-        grad_out[unit_rows(r, (orders[r][0] + 4 - k) % 4), lanes] = get_subs(ref, rows_here)
-
     def finish():
-        for r in (0, 1):
-            store(0, r, 0, whole_code.at[r])
-        for u, (mine, r) in enumerate(units):
-            gathered_again[u].wait_recv()
-            for k in range(1 - mine, 4):
-                store(mine, r, k, whole_in.at[mine, r, k])
+        for half in (1, 0):
+            mine = (core + half) % 2
+            lanes = aligned(channels(half), 128, 128)
+            for r in (0, 1):
+                for n in (0, 1):
+                    pl.when(mine == n)(gathered_again[2 * n + r].wait_recv)
+                for k in range(4):
+                    rows = unit_rows(r, (orders[r][0] + 4 - k) % 4)
+                    grad_out[rows, lanes] = get_subs(whole_in.at[mine, r, k], rows_here)
 
     scattered_again, gathered, gathered_again = {}, {}, {}
 

time: 40.2 us -> 40.2 us (level)
  no operation moved by 1% of the time
where the time goes in v11:
time: 40.2 us; the launch traced here: 40.1 us
  Pallas kernels  37.8 us (94%)
  local copies, waits for them, and re-layouts  1.71 us (4%)
  between operations  0.64 us (2%)
    pallas_call x1, Pallas kernels, shards(): pl.pallas_call(kernel, out_shape=(pltpu.VMEM((2, OWN, 2, PLANE), BF16), p...  37.8 us
    slice x1, local copies, waits for them, and re-layouts, shards(): return (both[0], both[1], grad[:ROWS].reshape(filters.shape))  0.97 us

profile of v11, /device:TPU:1, one launch (start us, length us, event | category | flops | bytes accessed | tf_op | source)
XLA Modules:
  0.0 40.1 jit_solution(16480820917483377615)
XLA Ops:
  0.6 37.8 %shard_map.58 = (bf16[2,32,2,512]{3,2,1,0:T(2,128)(2,1)S(1)}, f32[896,256]{1,0:T(8,128)S(1)}) custom-call(bf16[32,2,512]{2,1,0:T(2,128)(2,1)} %feat_hbm.1, bf16[32,2,512]{2,1,0:T(2,128)(2,1)} %cot_hbm.1, bf16[864,256]{1,0:T(8,128)(2,1)} %bitcast.7), custom_call_target="tpu_custom_call" | custom-call | tf_op jit(solution)/shard_map/pallas_call | solution.py:530
  38.4 0.7 %slice_bitcast_fusion = (bf16[32,2,512]{2,1,0:T(2,128)(2,1)}, bf16[32,2,512]{2,1,0:T(2,128)(2,1)}) fusion(bf16[2,32,2,512]{3,2,1,0:T(2,128)(2,1)S(1)} %get-tuple-element.5), kind=kLoop, calls=%fused_computation | loop fusion | bytes 262144 | tf_op jit(solution)/shard_map/squeeze | solution.py:579
  39.2 1.0 %slice.11 = f32[864,256]{1,0:T(8,128)} slice(f32[896,256]{1,0:T(8,128)S(1)} %get-tuple-element.6), slice={[0:864], [0:256]} | slice | bytes 1769472 | tf_op jit(solution)/shard_map/slice | solution.py:579
